TPU v7x, 256 devices: a whole 4x4x8 slice. The times are simulated.
256 devices in a mesh: section: 8 (over x_hi, y), expert: 32 (over z, x_lo, core).
Axes of the slice: x: 4 (x_hi: 2, x_lo: 2; x = x_hi * 2 + x_lo), y: 4, z: 8, core: 2. Of those that a mesh axis runs over, the one named last changes fastest.
Arguments:
- acts: bfloat16 [8, 8192, 2048], P('section', 'expert'), may hold values from -6 to 6
- grad_out: bfloat16 [8, 8192, 2048], P('section', 'expert'), may hold values from -6 to 6
- expert_of: int32 [8, 8192, 2], P('section', 'expert'), may hold values from 0 to 31, as said below
- slot_of: int32 [8, 8192, 2], P('section', 'expert'), may hold values from 0 to 1023, as said below
- source_row: int32 [8, 32, 1024], P('section', None, 'expert'), may hold values from -1 to 8191, as said below
- combine: bfloat16 [8, 8192, 2], P('section', 'expert'), may hold values from 0.099609375 to 1
- w_gate: bfloat16 [8, 32, 2048, 384], P('section', 'expert'), may hold values from -0.125 to 0.125
- w_up: bfloat16 [8, 32, 2048, 384], P('section', 'expert'), may hold values from -0.125 to 0.125
- w_down: bfloat16 [8, 32, 384, 2048], P('section', 'expert'), may hold values from -0.3125 to 0.3125
Outputs:
- grad_acts: bfloat16 [8, 8192, 2048], P('section', 'expert')
- grad_combine: bfloat16 [8, 8192, 2], P('section', 'expert')
- grad_gate: bfloat16 [8, 32, 2048, 384], P('section', 'expert')
- grad_up: bfloat16 [8, 32, 2048, 384], P('section', 'expert')
- grad_down: bfloat16 [8, 32, 384, 2048], P('section', 'expert')
Inputs may be any that keep to these rules, and one draw needn't show every extreme that they name: `expert_of`: each token names 2 different experts. Within the rows of one index of expert, no expert is named more than 32 times, and some expert exactly 32 times. `slot_of`: A token of the j-th block of 256 rows of a section takes a slot c of its expert with c // 32 = j; no two tokens share a slot; in every block some expert uses all 32 slots of that block. `source_row`: exactly the inverse of expert_of and slot_of: slot c of expert e holds the token that names e with slot c, or -1 where none does.
All inputs are finite; a program needn't handle non-finite values.
Results may differ from a plain program's by a relative error of at most 0.0065.
Values may be sent and summed in bfloat16 or wider, within the bound.
No kernel may reach another device: no remote copies, remote signals or barrier semaphores. Data moves between devices by JAX's collectives and lax.ppermute only.
A program may use at most 128 MiB of HBM per device.

v0:
```python
import jax
import jax.numpy as jnp
from jax import lax
from jax.sharding import PartitionSpec as P


def forward_rows(x_rows, weight_gate, weight_up, weight_down):
    pre_gate = jnp.dot(x_rows, weight_gate, preferred_element_type=jnp.float32)
    pre_up = jnp.dot(x_rows, weight_up, preferred_element_type=jnp.float32)
    sigmoid_gate = jax.nn.sigmoid(pre_gate)
    silu_gate = pre_gate * sigmoid_gate
    hidden = (silu_gate * pre_up).astype(jnp.bfloat16)
    expert_out = jnp.dot(hidden, weight_down, preferred_element_type=jnp.float32)
    return (pre_gate, pre_up, sigmoid_gate, silu_gate, hidden, expert_out)


def backward_rows(x_rows, g_rows, slot_weight, state, weight_gate, weight_up, weight_down):
    pre_gate, pre_up, sigmoid_gate, silu_gate, hidden, expert_out = state
    slot_score = jnp.sum(expert_out * g_rows.astype(jnp.float32), axis=1).astype(jnp.bfloat16)
    scaled = (slot_weight.astype(jnp.float32)[:, None] * g_rows.astype(jnp.float32)).astype(
        jnp.bfloat16
    )
    first = (((0,), (0,)), ((), ()))
    second = (((1,), (1,)), ((), ()))
    down_part = lax.dot_general(scaled, hidden, first, preferred_element_type=jnp.float32)
    grad_hidden = lax.dot_general(scaled, weight_down, second, preferred_element_type=jnp.float32)
    d_gate = (grad_hidden * pre_up * sigmoid_gate * (1.0 + pre_gate * (1.0 - sigmoid_gate))).astype(
        jnp.bfloat16
    )
    d_up = (grad_hidden * silu_gate).astype(jnp.bfloat16)
    gate_part = lax.dot_general(x_rows, d_gate, first, preferred_element_type=jnp.float32)
    up_part = lax.dot_general(x_rows, d_up, first, preferred_element_type=jnp.float32)
    dx_rows = lax.dot_general(d_gate, weight_gate, second, preferred_element_type=jnp.float32)
    dx_rows = dx_rows + lax.dot_general(d_up, weight_up, second, preferred_element_type=jnp.float32)
    return (
        dx_rows.astype(jnp.bfloat16),
        slot_score,
        gate_part.astype(jnp.bfloat16),
        up_part.astype(jnp.bfloat16),
        down_part.astype(jnp.bfloat16),
    )


def per_device(acts, grad_out, expert_of, slot_of, source_row, combine, w_gate, w_up, w_down):
    own_index = lax.axis_index("expert")
    tok_count = acts.shape[1]
    experts = source_row.shape[1]
    most = source_row.shape[2]
    slot_count = experts * most
    width = acts.shape[2]
    slot_rows = source_row[0]
    filled = slot_rows >= 0
    local_rows = jnp.where(filled, slot_rows - own_index * tok_count, 0)
    own_acts = acts[0]
    own_grad = grad_out[0]
    x_send = jnp.where(filled[:, :, None], own_acts[local_rows], jnp.zeros((), jnp.bfloat16))
    g_send = jnp.where(filled[:, :, None], own_grad[local_rows], jnp.zeros((), jnp.bfloat16))
    chosen = expert_of[0][local_rows] == jnp.arange(experts, dtype=jnp.int32)[:, None, None]
    picked = jnp.sum(jnp.where(chosen, combine[0][local_rows].astype(jnp.float32), 0.0), axis=2)
    slot_weight = jnp.where(filled, picked, 0.0).astype(jnp.bfloat16)
    weight_gate = w_gate[0, 0]
    weight_up = w_up[0, 0]
    weight_down = w_down[0, 0]
    x_recv, g_recv, w_recv = (
        lax.all_to_all(x_send, "expert", split_axis=0, concat_axis=0, tiled=True),
        lax.all_to_all(g_send, "expert", split_axis=0, concat_axis=0, tiled=True),
        lax.all_to_all(slot_weight, "expert", split_axis=0, concat_axis=0, tiled=True),
    )
    x_rows = x_recv.reshape(slot_count, width)
    state = forward_rows(x_rows, weight_gate, weight_up, weight_down)
    dx_rows, slot_score, gate_part, up_part, down_part = backward_rows(
        x_rows,
        g_recv.reshape(slot_count, width),
        w_recv.reshape(slot_count),
        state,
        weight_gate,
        weight_up,
        weight_down,
    )
    back_rows, back_score = (
        lax.all_to_all(
            dx_rows.reshape(experts, most, width), "expert", split_axis=0, concat_axis=0, tiled=True
        ),
        lax.all_to_all(
            slot_score.reshape(experts, most), "expert", split_axis=0, concat_axis=0, tiled=True
        ),
    )
    flat_index = expert_of[0] * most + slot_of[0] - own_index * most
    grad_acts = jnp.sum(
        back_rows.reshape(slot_count, width)[flat_index].astype(jnp.float32), axis=1
    ).astype(jnp.bfloat16)
    grad_combine = back_score.reshape(slot_count)[flat_index]
    stacked = jnp.stack([gate_part, up_part, down_part])
    spread = lax.all_to_all(stacked[None], "section", split_axis=2, concat_axis=0, tiled=True)
    paired = (spread.astype(jnp.float32) + spread[::-1].astype(jnp.float32)).astype(jnp.bfloat16)
    summed = lax.all_to_all(paired, "section", split_axis=0, concat_axis=2, tiled=True)[0]
    return (
        grad_acts[None],
        grad_combine[None],
        summed[0][None, None],
        summed[1][None, None],
        summed[2].T[None, None],
    )


def solution(mesh):
    return jax.shard_map(
        per_device,
        mesh=mesh,
        in_specs=(
            P("section", "expert", None),
            P("section", "expert", None),
            P("section", "expert", None),
            P("section", "expert", None),
            P("section", None, "expert"),
            P("section", "expert", None),
            P("section", "expert", None, None),
            P("section", "expert", None, None),
            P("section", "expert", None, None),
        ),
        out_specs=(
            P("section", "expert", None),
            P("section", "expert", None),
            P("section", "expert", None, None),
            P("section", "expert", None, None),
            P("section", "expert", None, None),
        ),
        check_vma=False,
    )
```

profile of v0, /device:TPU:2, one launch (start us, length us, event | category | flops | bytes accessed | tf_op | source)
XLA Modules:
  0.0 563.0 jit_solution(15947298491745135311)
XLA Ops:
  10.9 10.1 %all-to-all-start = ((bf16[32,1,32]{2,1,0:T(2,128)(2,1)}), bf16[32,1,32]{2,1,0:T(2,128)(2,1)S(1)}, u32[]{:S(2)}, u32[]{:S(2)}) async-start(bf16[32,1,32]{2,1,0:T(2,128)(2,1)} %copy.32), calls=%async_computation | async-start | bytes 32768 | tf_op jit(solution)/shard_map/all_to_all | solution.py:67
  21.7 6.0 %gather_fusion.3 = bf16[1024,2048]{1,0:T(8,128)(2,1)} fusion(bf16[256,2048]{1,0:T(8,128)(2,1)S(1)} %bitcast.90, s32[1024]{0:T(1024)S(1)} %broadcast_clamp_fusion), kind=kCustom, calls=%fused_computation.3 | custom fusion | bytes 8392704 | tf_op jit(solution)/shard_map/gather | solution.py:56
  27.7 10.2 %gather_fusion.2 = bf16[1024,2048]{1,0:T(8,128)(2,1)} fusion(bf16[256,2048]{1,0:T(8,128)(2,1)} %bitcast.91, s32[1024]{0:T(1024)S(1)} %broadcast_clamp_fusion), kind=kCustom, calls=%fused_computation.2 | custom fusion | bytes 8392704 | tf_op jit(solution)/shard_map/gather | solution.py:57
  37.9 5.8 %broadcast_select_fusion.1 = (bf16[32,32,2048]{2,1,0:T(8,128)(2,1)}, bf16[32,32,2048]{2,1,0:T(8,128)(2,1)}) fusion(bf16[32,32,2048]{2,1,0:T(8,128)(2,1)} %bitcast.96, pred[32,32]{1,0:T(8,128)(4,1)S(1)} %fusion.19, bf16[32,32,2048]{2,1,0:T(8,128)(2,1)} %bitcast.95), kind=kLoop, calls=%fused_computation.17 | loop fusion | flops 4194304 | bytes 16778240 | tf_op jit(solution)/shard_map/jit(_where)/select_n | solution.py:57
  43.7 104.7 %all_to_all.60 = bf16[32,32,2048]{2,1,0:T(8,128)(2,1)} all-to-all(bf16[32,32,2048]{2,1,0:T(8,128)(2,1)} %get-tuple-element.27), channel_id=1, replica_groups=mesh['section'=8,'expert'=32] {'expert'}, dimensions={0} | all-to-all | bytes 8388608 | tf_op jit(solution)/shard_map/all_to_all | solution.py:65
  148.4 5.6 %all-to-all-start.1 = ((bf16[32,32,2048]{2,1,0:T(8,128)(2,1)}), bf16[32,32,2048]{2,1,0:T(8,128)(2,1)}, u32[]{:S(2)}, u32[]{:S(2)}) async-start(bf16[32,32,2048]{2,1,0:T(8,128)(2,1)} %get-tuple-element.26), calls=%async_computation.1 | async-start | bytes 8388608 | tf_op jit(solution)/shard_map/all_to_all | solution.py:66
  154.2 5.7 %fusion.8 = f32[1024,384]{1,0:T(8,128)} fusion(bf16[1024,2048]{1,0:T(8,128)(2,1)} %bitcast.99, bf16[1,1,2048,384]{3,2,1,0:T(8,128)(2,1)S(1)} %copy-done.4), kind=kOutput, calls=%fused_computation.26 | convolution fusion | flops 1610612736 | bytes 7340032 | tf_op jit(solution)/shard_map/dot_general | solution.py:8
  159.9 88.1 %all-to-all-done.1 = bf16[32,32,2048]{2,1,0:T(8,128)(2,1)} async-done(((bf16[32,32,2048]{2,1,0:T(8,128)(2,1)}), bf16[32,32,2048]{2,1,0:T(8,128)(2,1)}, u32[]{:S(2)}, u32[]{:S(2)}) %all-to-all-start.1) | async-done | bytes 4194336 | tf_op jit(solution)/shard_map/all_to_all | solution.py:66
  253.7 4.1 multiply_convert_fusion
  264.3 4.6 fusion.1
  269.6 6.8 %all-to-all-start.4 = ((bf16[32,1,32]{2,1,0:T(2,128)(2,1)}), bf16[32,1,32]{2,1,0:T(2,128)(2,1)S(1)}, u32[]{:S(2)}, u32[]{:S(2)}) async-start(bf16[32,1,32]{2,1,0:T(2,128)(2,1)} %convert_element_type.121), calls=%async_computation.4 | async-start | bytes 32768 | tf_op jit(solution)/shard_map/all_to_all | solution.py:84
  276.4 4.9 fusion.3
  284.5 31.9 %copy.35 = bf16[1,3,2048,384]{3,1,0,2:T(4,128)(2,1)} copy(bf16[1,3,2048,384]{3,2,1,0:T(8,128)(2,1)S(1)} %maximum_bitcast_fusion) | data formatting | bytes 9437184 | tf_op jit(solution)/shard_map/broadcast_in_dim | solution.py:94
  316.4 6.3 %all-to-all-start.5 = ((bf16[1,3,2048,384]{3,1,0,2:T(4,128)(2,1)}), bf16[1,3,2048,384]{3,1,0,2:T(4,128)(2,1)}, u32[]{:S(2)}, u32[]{:S(2)}) async-start(bf16[1,3,2048,384]{3,1,0,2:T(4,128)(2,1)} %copy.35), calls=%async_computation.5 | async-start | bytes 12582912 | tf_op jit(solution)/shard_map/all_to_all | solution.py:94
  326.3 4.3 add_convert_fusion.1
  330.7 63.8 %all-to-all-done.5 = bf16[1,3,2048,384]{3,1,0,2:T(4,128)(2,1)} async-done(((bf16[1,3,2048,384]{3,1,0,2:T(4,128)(2,1)}), bf16[1,3,2048,384]{3,1,0,2:T(4,128)(2,1)}, u32[]{:S(2)}, u32[]{:S(2)}) %all-to-all-start.5) | async-done | bytes 4718624 | tf_op jit(solution)/shard_map/all_to_all | solution.py:94
  394.4 8.4 %all-to-all-start.3 = ((bf16[32,32,2048]{2,1,0:T(8,128)(2,1)}), bf16[32,32,2048]{2,1,0:T(8,128)(2,1)}, u32[]{:S(2)}, u32[]{:S(2)}) async-start(bf16[32,32,2048]{2,1,0:T(8,128)(2,1)} %bitcast.97), calls=%async_computation.3 | async-start | bytes 8388608 | tf_op jit(solution)/shard_map/all_to_all | solution.py:81
  409.7 87.2 %all-to-all-done.3 = bf16[32,32,2048]{2,1,0:T(8,128)(2,1)} async-done(((bf16[32,32,2048]{2,1,0:T(8,128)(2,1)}), bf16[32,32,2048]{2,1,0:T(8,128)(2,1)}, u32[]{:S(2)}, u32[]{:S(2)}) %all-to-all-start.3) | async-done | bytes 4194336 | tf_op jit(solution)/shard_map/all_to_all | solution.py:81
  496.9 4.8 all-to-all-start.6
  506.5 8.0 %gather_fusion.4 = bf16[512,2048]{1,0:T(8,128)(2,1)} fusion(bf16[1024,2048]{1,0:T(8,128)(2,1)} %bitcast.19, s32[1024]{0:T(1024)S(1)} %pad_clamp_fusion), kind=kCustom, calls=%fused_computation.4 | custom fusion | bytes 4196352 | tf_op jit(solution)/shard_map/gather | solution.py:90
  514.5 4.4 reshape.213
  518.9 7.7 %reduce_sum.34 = bf16[256,2048]{1,0:T(8,128)(2,1)} reduce(bf16[256,2,2048]{2,1,0:T(2,128)(2,1)} %reshape.213, bf16[]{:T(256)} %constant.12.clone.1), dimensions={1}, to_apply=%region_1.2 | reduce | flops 524288 | bytes 3145730 | tf_op jit(solution)/shard_map/reduce_sum | solution.py:89
  526.5 30.0 %all-to-all-done.6 = bf16[8,3,256,384]{3,2,1,0:T(8,128)(2,1)} async-done(((bf16[8,3,256,384]{3,2,1,0:T(8,128)(2,1)}), bf16[8,3,256,384]{3,2,1,0:T(8,128)(2,1)}, u32[]{:S(2)}, u32[]{:S(2)}) %all-to-all-start.6) | async-done | bytes 4718624 | tf_op jit(solution)/shard_map/all_to_all | solution.py:96
  556.5 4.7 fusion.20
  (60 shorter events, 43.9 us)
Async XLA Ops:
  0.6 252.8 %copy-start = (bf16[1,1,2048,384]{3,2,1,0:T(8,128)(2,1)S(1)}, bf16[1,1,2048,384]{3,2,1,0:T(8,128)(2,1)}, u32[]{:S(2)}) copy-start(bf16[1,1,2048,384]{3,2,1,0:T(8,128)(2,1)} %param.16) | copy-start | bytes 4718596
  0.6 21.0 %copy-start.1 = (bf16[1,256,2048]{2,1,0:T(8,128)(2,1)S(1)}, bf16[1,256,2048]{2,1,0:T(8,128)(2,1)}, u32[]{:S(2)}) copy-start(bf16[1,256,2048]{2,1,0:T(8,128)(2,1)} %param.9) | copy-start | bytes 3145732
  10.9 32.8 %all-to-all-start = ((bf16[32,1,32]{2,1,0:T(2,128)(2,1)}), bf16[32,1,32]{2,1,0:T(2,128)(2,1)S(1)}, u32[]{:S(2)}, u32[]{:S(2)}) async-start(bf16[32,1,32]{2,1,0:T(2,128)(2,1)} %copy.32), calls=%async_computation | async-start | bytes 32768 | tf_op jit(solution)/shard_map/all_to_all | solution.py:67
  148.4 5.8 %copy-start.4 = (bf16[1,1,2048,384]{3,2,1,0:T(8,128)(2,1)S(1)}, bf16[1,1,2048,384]{3,2,1,0:T(8,128)(2,1)}, u32[]{:S(2)}) copy-start(bf16[1,1,2048,384]{3,2,1,0:T(8,128)(2,1)} %param.15) | copy-start | bytes 4718596
  148.4 99.6 %all-to-all-start.1 = ((bf16[32,32,2048]{2,1,0:T(8,128)(2,1)}), bf16[32,32,2048]{2,1,0:T(8,128)(2,1)}, u32[]{:S(2)}, u32[]{:S(2)}) async-start(bf16[32,32,2048]{2,1,0:T(8,128)(2,1)} %get-tuple-element.26), calls=%async_computation.1 | async-start | bytes 8388608 | tf_op jit(solution)/shard_map/all_to_all | solution.py:66
  248.0 3.1 copy-start.10
  251.0 2.4 copy-start.2
  251.1 2.7 copy-start.11
  269.6 46.8 %all-to-all-start.4 = ((bf16[32,1,32]{2,1,0:T(2,128)(2,1)}), bf16[32,1,32]{2,1,0:T(2,128)(2,1)S(1)}, u32[]{:S(2)}, u32[]{:S(2)}) async-start(bf16[32,1,32]{2,1,0:T(2,128)(2,1)} %convert_element_type.121), calls=%async_computation.4 | async-start | bytes 32768 | tf_op jit(solution)/shard_map/all_to_all | solution.py:84
  276.4 5.0 copy-start.3
  276.4 5.0 copy-start.6
  281.4 2.5 copy-start.5
  316.4 78.0 %all-to-all-start.5 = ((bf16[1,3,2048,384]{3,1,0,2:T(4,128)(2,1)}), bf16[1,3,2048,384]{3,1,0,2:T(4,128)(2,1)}, u32[]{:S(2)}, u32[]{:S(2)}) async-start(bf16[1,3,2048,384]{3,1,0,2:T(4,128)(2,1)} %copy.35), calls=%async_computation.5 | async-start | bytes 12582912 | tf_op jit(solution)/shard_map/all_to_all | solution.py:94
  322.7 3.6 copy-start.7
  394.4 102.5 %all-to-all-start.3 = ((bf16[32,32,2048]{2,1,0:T(8,128)(2,1)}), bf16[32,32,2048]{2,1,0:T(8,128)(2,1)}, u32[]{:S(2)}, u32[]{:S(2)}) async-start(bf16[32,32,2048]{2,1,0:T(8,128)(2,1)} %bitcast.97), calls=%async_computation.3 | async-start | bytes 8388608 | tf_op jit(solution)/shard_map/all_to_all | solution.py:81
  409.7 92.0 %copy-start.8 = (s32[1,256,2]{1,2,0:T(2,128)S(1)}, s32[1,256,2]{1,2,0:T(2,128)}, u32[]{:S(2)}) copy-start(s32[1,256,2]{1,2,0:T(2,128)} %param.11) | copy-start | bytes 6148
  409.7 92.0 %copy-start.9 = (s32[1,256,2]{1,2,0:T(2,128)S(1)}, s32[1,256,2]{1,2,0:T(2,128)}, u32[]{:S(2)}) copy-start(s32[1,256,2]{1,2,0:T(2,128)} %param.12) | copy-start | bytes 6148
  496.9 59.6 %all-to-all-start.6 = ((bf16[8,3,256,384]{3,2,1,0:T(8,128)(2,1)}), bf16[8,3,256,384]{3,2,1,0:T(8,128)(2,1)}, u32[]{:S(2)}, u32[]{:S(2)}) async-start(bf16[8,3,256,384]{3,2,1,0:T(8,128)(2,1)} %add_convert_fusion), calls=%async_computation.6 | async-start | bytes 9437184 | tf_op jit(solution)/shard_map/all_to_all | solution.py:96
where the time goes:
time: 569 us; the launch traced here: 563 us
  waiting for transfers between devices  269 us (47%)
  blocking collectives  105 us (18%)
  local copies, waits for them, and re-layouts  84.7 us (15%)
  starting transfers between devices  41.9 us (7%)
  matrix products  35.6 us (6%)
  other arithmetic  25.8 us (5%)
    all_to_all x1, blocking collectives, per_device(): lax.all_to_all(x_send, 'expert', split_axis=0, concat_axis=0, tiled=True)  105 us
    all_to_all x1, waiting for transfers between devices, per_device(): lax.all_to_all(g_send, 'expert', split_axis=0, concat_axis=0, tiled=True)  88.1 us
    all_to_all x1, waiting for transfers between devices, per_device(): lax.all_to_all(dx_rows.reshape(experts, most, width), 'expert', split_axi...  87.2 us
    all_to_all x1, waiting for transfers between devices, per_device(): lax.all_to_all(stacked[None], 'section', split_axis=2, concat_axis=0, til...  63.8 us
    broadcast_in_dim x1, local copies, waits for them, and re-layouts, per_device(): stacked[None]  31.9 us
    all_to_all x1, waiting for transfers between devices, per_device(): lax.all_to_all(paired, 'section', split_axis=0, concat_axis=2, tiled=True)  30 us
    gather x2, local copies, waits for them, and re-layouts, per_device(): back_rows.reshape(slot_count, width)[flat_index].astype(jnp.float32)  12.4 us
  transfers between devices with their start and end apart: 6, of which 4 were waited for; matrix products, arithmetic and copies ran while one was open for 19% of the time, Pallas kernels for 0%

commit v1 on v0

v1 whole, which is shorter than its diff:
```python
import jax
import jax.numpy as jnp
from jax import lax
from jax.experimental import pallas as pl
from jax.experimental.pallas import tpu as pltpu
from jax.sharding import PartitionSpec as P

BF = jnp.bfloat16
F32 = jnp.float32
RING = 8
LANES = 4


def ring_step(step):
    return [
        (z * LANES + lane, ((z + step) % RING) * LANES + lane)
        for z in range(RING)
        for lane in range(LANES)
    ]


PLANE_GROUPS = [[z * LANES + lane for lane in range(LANES)] for z in range(RING)]
COLUMN_GROUPS = [
    [z * LANES + 2 * col + core for z in range(RING) for core in range(2)] for col in range(2)
]
ACROSS = [(e, e ^ 2) for e in range(RING * LANES)]
FIRST = (((0,), (0,)), ((), ()))
SECOND = (((1,), (1,)), ((), ()))


def dot(a, b, dims=(((1,), (0,)), ((), ()))):
    return lax.dot_general(a, b, dims, preferred_element_type=F32)


ROUTE_ROWS = 16
SCORE = 128
ANYWHERE = pl.BlockSpec(memory_space=pl.ANY)
WHOLE = pl.BlockSpec(memory_space=pltpu.VMEM)
LIGHT = pl.CostEstimate(flops=1, bytes_accessed=1, transcendentals=0)
PARAMS = pltpu.CompilerParams(vmem_limit_bytes=63 * 1024 * 1024)
TILE = 512


def route_rows(acts, source_row, expert_of, combine, me):
    tok, width = acts.shape
    most = source_row.shape[1]
    slots = LANES * most

    def body(me_ref, acts_ref, source_ref, expert_ref, combine_ref, out_ref, table_ref):
        own = me_ref[0]
        own_z = own // LANES
        out_ref[:tok, :] = acts_ref[...]
        names = lax.broadcasted_iota(jnp.int32, (tok, slots), 0)
        which = lax.broadcasted_iota(jnp.int32, (1, slots), 1) // most
        wide = combine_ref[...].astype(F32)
        for p in range(RING):
            plane = lax.rem(own_z + p, RING) * LANES
            for r in range(LANES):
                row = source_ref[pl.ds(plane + r, 1), :]
                row = jnp.where(row >= 0, row - own * tok, -1)
                table_ref[p : p + 1, r * most : (r + 1) * most] = row.astype(F32)
            hot = names == table_ref[p : p + 1, :].astype(jnp.int32)
            expert = plane + which
            weight = jnp.zeros((tok, slots), F32)
            for k in range(2):
                chosen = expert_ref[:, k : k + 1] == expert
                weight = weight + jnp.where(chosen, wide[:, k : k + 1], 0.0)
            weight = jnp.sum(jnp.where(hot, weight, 0.0), axis=0, keepdims=True)
            table_ref[RING + p : RING + p + 1, :] = weight
        out_ref[tok:, :] = jnp.zeros((ROUTE_ROWS, width), BF)
        out_ref[tok:, :slots] = table_ref[...].astype(BF)

    return pl.pallas_call(
        body,
        out_shape=jax.ShapeDtypeStruct((tok + ROUTE_ROWS, width), BF),
        in_specs=[pl.BlockSpec(memory_space=pltpu.SMEM)] + [WHOLE] * 4,
        out_specs=WHOLE,
        scratch_shapes=[pltpu.VMEM((ROUTE_ROWS, slots), F32)],
        cost_estimate=LIGHT,
        compiler_params=PARAMS,
    )(me.reshape(1), acts, source_row, expert_of, combine)


def pick(route, plane, x_ref, g_ref):
    tok = g_ref.shape[0]
    names = route[plane : plane + 1, :].astype(jnp.int32)
    index = lax.broadcasted_iota(jnp.int32, (tok, names.shape[1]), 0)
    hot = index == names
    weight = jnp.where(hot, route[RING + plane : RING + plane + 1, :], 0.0).astype(BF)
    x = dot(hot.astype(F32).astype(BF), x_ref[:tok, :], FIRST).astype(BF)
    return x, dot(weight, g_ref[...], FIRST).astype(BF)


def pick_call(body, sources, out_rows, after):
    tok, width = sources[0][1].shape
    count = len(sources)
    slots = LANES * 32

    def inner(*refs):
        routes = [r[:, :slots].astype(F32) for r in refs[:count]]
        outs = refs[3 * count + len(after) :]
        body(routes, refs[count : 2 * count], refs[2 * count : 3 * count], outs)

    def columns(rows):
        return pl.BlockSpec((rows, TILE), lambda i: (0, i))

    xs = [x for x, _ in sources]
    gs = [g for _, g in sources]
    return pl.pallas_call(
        inner,
        grid=(width // TILE,),
        out_shape=[jax.ShapeDtypeStruct((n, width), BF) for n in out_rows],
        in_specs=[pl.BlockSpec((ROUTE_ROWS, TILE), lambda i: (tok // ROUTE_ROWS, 0))] * count
        + [columns(tok + ROUTE_ROWS)] * count
        + [columns(tok)] * count
        + [ANYWHERE] * len(after),
        out_specs=[columns(n) for n in out_rows],
        cost_estimate=LIGHT,
        compiler_params=PARAMS,
    )(*xs, *xs, *gs, *after)


def pick_lanes(sources, planes, most, after=()):
    size = len(sources) * 2 * most

    def body(routes, x_refs, g_refs, outs):
        for i in range(len(sources)):
            for t, rows in enumerate(pick(routes[i], planes[i], x_refs[i], g_refs[i])):
                for r in range(LANES):
                    at = r * size + (2 * i + t) * most
                    outs[0][at : at + most, :] = rows[r * most : (r + 1) * most]

    return pick_call(body, sources, [LANES * size], after)[0]


def pick_onward(sources, planes, most, after=()):
    half = most // 2
    low = 2 * LANES * most

    def body(routes, x_refs, g_refs, outs):
        for d in range(2):
            for t, rows in enumerate(pick(routes[d], planes[d][0], x_refs[d], g_refs[d])):
                for r in range(LANES):
                    to = (2 * r + t) * most
                    outs[d][to : to + most, :] = rows[r * most : (r + 1) * most]
            for t, rows in enumerate(pick(routes[d], planes[d][1], x_refs[d], g_refs[d])):
                for r in range(LANES):
                    to, at = low + (2 * r + t) * half, r * most + d * half
                    outs[d][to : to + half, :] = rows[at : at + half]

    return pick_call(body, sources, [low + low // 2] * 2, after)


def spread(up, down, rows, onward, after=()):
    width = up.shape[1]
    rest = up.shape[0] - rows
    size = rows // LANES

    def body(up_ref, down_ref, *refs):
        outs = refs[len(after) :]
        for r in range(LANES):
            for i, ref in enumerate((up_ref, down_ref)):
                to = (2 * r + i) * size
                outs[0][to : to + size, :] = ref[r * size : (r + 1) * size, :]
        if onward:
            outs[1][...] = up_ref[rows:, :]
            outs[2][...] = down_ref[rows:, :]

    shapes = [2 * rows] + [rest] * (2 * onward)

    def columns(count):
        return pl.BlockSpec((count, TILE), lambda i: (0, i))

    return pl.pallas_call(
        body,
        grid=(width // TILE,),
        out_shape=[jax.ShapeDtypeStruct((n, width), BF) for n in shapes],
        in_specs=[columns(up.shape[0])] * 2 + [ANYWHERE] * len(after),
        out_specs=[columns(n) for n in shapes],
        cost_estimate=LIGHT,
        compiler_params=PARAMS,
    )(up, down, *after)


def collect(back, place, lane_info, width):
    slots = back.shape[0]
    tok = place.shape[0]

    def body(info_ref, place_ref, back_ref, out_ref):
        slot = lax.broadcasted_iota(jnp.int32, (tok, slots), 1)
        most = 32
        expert = (slot // (4 * most)) * LANES + info_ref[0] * 2 + (slot // (2 * most)) % 2
        wanted = expert * most + slot % most
        wanted = jnp.where((slot // most) % 2 == info_ref[1], wanted, -1)
        hots = [place_ref[:, k : k + 1] == wanted for k in range(2)]
        hots = [h.astype(F32) for h in hots]
        both = (hots[0] + hots[1]).astype(BF)
        out_ref[:, :width] = dot(both, back_ref[:, :width]).astype(out_ref.dtype)
        tail = back_ref[:, width:]
        scores = [dot(h.astype(BF), tail) for h in hots]
        at = lax.broadcasted_iota(jnp.int32, scores[0].shape, 1)
        kept = jnp.where(at < 2, scores[0], jnp.where(at < 4, scores[1], 0.0))
        out_ref[:, width:] = kept.astype(out_ref.dtype)

    return pl.pallas_call(
        body,
        out_shape=jax.ShapeDtypeStruct((tok, back.shape[1]), BF),
        in_specs=[pl.BlockSpec(memory_space=pltpu.SMEM), WHOLE, WHOLE],
        out_specs=WHOLE,
        cost_estimate=LIGHT,
        compiler_params=PARAMS,
    )(jnp.stack(lane_info), place, back)


def chunk_grads(block, run, start, total_rows, places, shared, weights, after=()):
    rows, width = block.shape
    rows = rows // LANES
    size = rows // 2
    count = LANES * size
    ff = weights[0].shape[1]
    most = 32
    runs = size // run
    n_in = 2 + 3 + len(after) + len(shared)

    def body(*refs):
        place_ref = refs[0]
        gate_ref, up_ref, down_ref = refs[2:5]
        outs = refs[n_in : n_in + 5]
        x, g, hid, d, dx, wg, wu, wd, sems, out_sems = refs[n_in + 5 :]
        loads = [
            pltpu.make_async_copy(gate_ref, wg, sems.at[0]),
            pltpu.make_async_copy(up_ref, wu, sems.at[1]),
            pltpu.make_async_copy(down_ref, wd, sems.at[2]),
        ]
        pieces = []
        for t, into in enumerate((x, g)):
            for r in range(LANES):
                for i in range(runs):
                    pieces.append(
                        pltpu.make_async_copy(
                            refs[1].at[pl.ds(r * rows + (2 * i + t) * run, run), :],
                            into.at[pl.ds(r * size + i * run, run), :],
                            sems.at[3 + len(pieces)],
                        )
                    )
        split = len(pieces) // 2
        for copy in pieces[:split] + loads[:2] + pieces[split:] + loads[2:]:
            copy.start()
        stores = []

        def store(part, ref):
            stores.append(pltpu.make_async_copy(part, ref, out_sems.at[len(stores)]))
            stores[-1].start()

        mine = pl.ds(start, count)
        for copy in pieces[:split]:
            copy.wait()
        store(x, outs[0].at[mine, :])
        loads[0].wait()
        pre_gate = dot(x[...], wg[...])
        loads[1].wait()
        pre_up = dot(x[...], wu[...])
        sig = jax.nn.sigmoid(pre_gate)
        silu = pre_gate * sig
        hidden = silu * pre_up
        hid[...] = hidden.astype(BF)
        store(hid, outs[2].at[mine, :])
        for copy in pieces[split:]:
            copy.wait()
        store(g, outs[1].at[mine, :])
        loads[2].wait()
        grad_hidden = dot(g[...], wd[...], SECOND)
        score = jnp.sum(hid[...].astype(F32) * grad_hidden, axis=1, keepdims=True)
        high = score.astype(BF).astype(F32)
        at = lax.broadcasted_iota(jnp.int32, (count, SCORE), 1)
        tail = jnp.where(at % 2 == 0, high, score - high)
        dx[:, width:] = jnp.where(at < 4, tail, 0.0).astype(BF)
        d_gate = (grad_hidden * pre_up * sig * (1.0 + pre_gate * (1.0 - sig))).astype(BF)
        d_up = (grad_hidden * silu).astype(BF)
        d[:, :ff] = d_gate
        d[:, ff:] = d_up
        store(d, outs[3].at[mine, :])
        back = dot(d_gate, wg[...], SECOND) + dot(d_up, wu[...], SECOND)
        dx[:, :width] = back.astype(BF)
        for b in range(count // most):
            to = pl.multiple_of(place_ref[b], most)
            store(dx.at[pl.ds(b * most, most), :], outs[4].at[pl.ds(to, most), :])
        for copy in stores:
            copy.wait()

    shapes = [width, width, ff, 2 * ff, width + SCORE]
    first = 5 + len(after)
    return pl.pallas_call(
        body,
        out_shape=[jax.ShapeDtypeStruct((total_rows, n), BF) for n in shapes],
        in_specs=[pl.BlockSpec(memory_space=pltpu.SMEM)] + [ANYWHERE] * (n_in - 1),
        out_specs=[ANYWHERE] * 5,
        input_output_aliases={first + i: i for i in range(len(shared))},
        scratch_shapes=[
            pltpu.VMEM((count, width), BF),
            pltpu.VMEM((count, width), BF),
            pltpu.VMEM((count, ff), BF),
            pltpu.VMEM((count, 2 * ff), BF),
            pltpu.VMEM((count, width + SCORE), BF),
            pltpu.VMEM((width, ff), BF),
            pltpu.VMEM((width, ff), BF),
            pltpu.VMEM((ff, width), BF),
            pltpu.SemaphoreType.DMA((3 + 2 * LANES * runs,)),
            pltpu.SemaphoreType.DMA((4 + count // most,)),
        ],
        cost_estimate=LIGHT,
        compiler_params=PARAMS,
    )(places, block, *weights, *after, *shared)


def weight_grads(left, right, across, after=()):
    count = left.shape[0]
    shape = (left.shape[1], right.shape[1])
    tile = 512

    def body(left_ref, right_ref, *refs):
        refs[-1][...] = dot(left_ref[...], right_ref[...], FIRST).astype(BF)

    def fixed(a):
        return pl.BlockSpec(a.shape, lambda i: (0, 0))

    moving = pl.BlockSpec((count, tile), lambda i: (0, i))

    return pl.pallas_call(
        body,
        grid=(shape[1] // tile if across else shape[0] // tile,),
        out_shape=jax.ShapeDtypeStruct(shape, BF),
        in_specs=([fixed(left), moving] if across else [moving, fixed(right)])
        + [ANYWHERE] * len(after),
        out_specs=pl.BlockSpec((shape[0], tile), lambda i: (0, i))
        if across
        else pl.BlockSpec((tile, shape[1]), lambda i: (i, 0)),
        cost_estimate=LIGHT,
        compiler_params=PARAMS,
    )(left, right, *after)


def total(a, b, parts, after):
    rows, columns = a.shape
    tile, part = rows // 4, columns // parts

    def body(a_ref, b_ref, *refs):
        both = (a_ref[...].astype(F32) + b_ref[...].astype(F32)).astype(BF)
        for i in range(parts):
            refs[len(after) + i][...] = both[:, i * part : (i + 1) * part]

    def block(count):
        return pl.BlockSpec((tile, count), lambda i: (i, 0))

    return pl.pallas_call(
        body,
        grid=(4,),
        out_shape=[jax.ShapeDtypeStruct((rows, part), BF)] * parts,
        in_specs=[block(columns)] * 2 + [ANYWHERE] * len(after),
        out_specs=[block(part)] * parts,
        cost_estimate=LIGHT,
        compiler_params=PARAMS,
    )(a, b, *after)


def per_device(acts, grad_out, expert_of, slot_of, source_row, combine, w_gate, w_up, w_down):
    me = lax.axis_index("expert")
    z = me // LANES
    col = (me // 2) % 2
    tok = acts.shape[1]
    width = acts.shape[2]
    experts = source_row.shape[1]
    most = source_row.shape[2]
    sections = lax.axis_size("section")
    weight_gate = w_gate[0, 0]
    weight_up = w_up[0, 0]
    weight_down = w_down[0, 0]
    up_ring = ring_step(1)
    down_ring = ring_step(-1)

    place = expert_of[0] * most + (slot_of[0] - me * most)
    place_across = lax.ppermute(place, "expert", ACROSS)
    routed = route_rows(acts[0], source_row[0], expert_of[0], combine[0], me)
    own = (routed, grad_out[0])
    plus1 = [lax.ppermute(t, "expert", up_ring) for t in own]
    minus1 = [lax.ppermute(t, "expert", down_ring) for t in own]
    plus2 = [lax.ppermute(t, "expert", up_ring) for t in plus1]
    minus2 = [lax.ppermute(t, "expert", down_ring) for t in minus1]

    def exchange(block):
        return lax.all_to_all(
            block, "expert", 0, 0, tiled=True, axis_index_groups=PLANE_GROUPS
        )

    slot_count = experts * most
    offsets_of = ((0,), (-1, 1), (-2, 2), (-3, 3), (4,))
    starts = [b * LANES * most for b in (0, 1, 3, 5, 7)]

    def places(offsets):
        found = []
        for other in range(LANES):
            for o in offsets:
                ring = (z + o + RING) % RING
                found.append(((ring * 2 + other % 2) * 2 + other // 2) * most)
        return jnp.stack(found).astype(jnp.int32)

    expert_weights = (weight_gate, weight_up, weight_down)

    def work(i, blocks, run, shared, after=()):
        return chunk_grads(
            blocks, run, starts[i], slot_count, places(offsets_of[i]), shared, expert_weights, after
        )

    own_out = pick_lanes([own], [0], most, after=[place_across])
    here_rows = exchange(own_out)
    shared = work(0, here_rows, most, [])
    near_out = pick_lanes(
        [plus1, minus1], [1, RING - 1], most, after=[shared[4], plus2[0], minus2[0]]
    )
    near = exchange(near_out)
    onward_up, onward_down = pick_onward(
        [plus2, minus2], [[3, 4], [RING - 3, RING - 4]], most, after=[near_out]
    )
    plus3 = lax.ppermute(onward_up, "expert", up_ring)
    minus3 = lax.ppermute(onward_down, "expert", down_ring)
    mid_out = pick_lanes([plus2, minus2], [2, RING - 2], most, after=[onward_up])
    mid = exchange(mid_out)
    shared = work(1, near, most, shared, after=[mid_out])
    far_out, last_up, last_down = spread(
        plus3, minus3, 2 * LANES * most, True, after=[shared[4]]
    )
    plus4 = lax.ppermute(last_up, "expert", up_ring)
    minus4 = lax.ppermute(last_down, "expert", down_ring)
    far = exchange(far_out)
    shared = work(2, mid, most, shared, after=[far_out])
    (last_out,) = spread(plus4, minus4, LANES * most, False, after=[shared[4]])
    last = exchange(last_out)
    shared = work(3, far, most, shared, after=[last_out])
    shared = work(4, last, most // 2, shared)

    x_all, g_all, hidden, d_rows, dx = shared
    down_part = weight_grads(hidden, g_all, True)
    in_parts = weight_grads(x_all, d_rows, False, after=[down_part])
    mirror = [(s, sections - 1 - s) for s in range(sections)]
    down_far = lax.ppermute(down_part, "section", mirror)
    in_far = lax.ppermute(in_parts, "section", mirror)

    back = lax.all_to_all(
        dx.reshape(2 * RING, 2 * most, width + SCORE),
        "expert",
        0,
        0,
        tiled=True,
        axis_index_groups=COLUMN_GROUPS,
    ).reshape(-1, width + SCORE)
    leaving = collect(back, place_across, [col, 1 - col], width)
    away = lax.ppermute(leaving, "expert", ACROSS)
    here = collect(back, place, [col, col], width)
    both = here.astype(F32) + away.astype(F32)
    grad_acts = both[:, :width].astype(BF)
    found = jnp.stack([both[:, width + 2 * k] + both[:, width + 2 * k + 1] for k in range(2)], 1)
    grad_combine = (found / combine[0].astype(F32)).astype(BF)
    (grad_down,) = total(down_part, down_far, 1, [leaving])
    grad_gate, grad_up = total(in_parts, in_far, 2, [grad_down])
    return (
        grad_acts[None],
        grad_combine[None],
        grad_gate[None, None],
        grad_up[None, None],
        grad_down[None, None],
    )


def solution(mesh):
    return jax.shard_map(
        per_device,
        mesh=mesh,
        in_specs=(
            P("section", "expert", None),
            P("section", "expert", None),
            P("section", "expert", None),
            P("section", "expert", None),
            P("section", None, "expert"),
            P("section", "expert", None),
            P("section", "expert", None, None),
            P("section", "expert", None, None),
            P("section", "expert", None, None),
        ),
        out_specs=(
            P("section", "expert", None),
            P("section", "expert", None),
            P("section", "expert", None, None),
            P("section", "expert", None, None),
            P("section", "expert", None, None),
        ),
        check_vma=False,
    )
```

time: 569 us -> 382 us (0.67)
  blocking collectives: 105 us -> 0 us
  Pallas kernels: 0 us -> 96.1 us
  local copies, waits for them, and re-layouts: 84.7 us -> 7.58 us
  waiting for transfers between devices: 269 us -> 210 us
  matrix products: 35.6 us -> 0 us
  other arithmetic: 25.8 us -> 5.09 us
  starting transfers between devices: 41.9 us -> 60.4 us
    all_to_all x6, waiting for transfers between devices: 269 us -> 102 us  [the longest x1 80.8 us: per_device(): lax.all_to_all(dx.reshape(2 * RING, 2 * most, width + SCORE), 'expert', 0...]
    ppermute x0 -> x16, waiting for transfers between devices: none -> 108 us  [the longest x2 34.2 us: per_device(): plus1 = [lax.ppermute(t, 'expert', up_ring) for t in own]]
    all_to_all x1 -> x0, blocking collectives: 105 us -> none  [per_device(): lax.all_to_all(x_send, 'expert', split_axis=0, concat_axis=0, tiled=True)]
    pallas_call x0 -> x18, Pallas kernels: none -> 96.1 us  [the longest x5 34.9 us: chunk_grads(): pl.pallas_call(body, out_shape=[jax.ShapeDtypeStruct((total_rows, n), BF)...]
    gather x7 -> x0, local copies, waits for them, and re-layouts: 38.1 us -> none  [the longest x2 12.4 us: per_device(): back_rows.reshape(slot_count, width)[flat_index].astype(jnp.float32)]
    dot_general x9 -> x0, matrix products: 35.6 us -> none  [the longest x1 5.66 us: forward_rows(): pre_gate = jnp.dot(x_rows, weight_gate, preferred_element_type=jnp.float32)]
    broadcast_in_dim x2 -> x1, local copies, waits for them, and re-layouts: 32 us -> 1.13 us  [per_device(): grad_acts[None]]
    ppermute x0 -> x16, starting transfers between devices: none -> 30 us  [the longest x2 7.17 us: per_device(): minus1 = [lax.ppermute(t, 'expert', down_ring) for t in own]]
  transfers between devices with their start and end apart: 6 -> 22, of which waited for: 4 -> 13; matrix products, arithmetic and copies ran while one was open for 19% -> 1% of each run, Pallas kernels for 0% -> 22%
where the time goes in v1:
time: 382 us; the launch traced here: 380 us
  waiting for transfers between devices  210 us (55%)
  Pallas kernels  96.1 us (25%)
  starting transfers between devices  60.4 us (16%)
  local copies, waits for them, and re-layouts  7.58 us (2%)
  other arithmetic  5.09 us (1%)
    all_to_all x1, waiting for transfers between devices, per_device(): lax.all_to_all(dx.reshape(2 * RING, 2 * most, width + SCORE), 'expert', 0...  80.8 us
    pallas_call x5, Pallas kernels, chunk_grads(): pl.pallas_call(body, out_shape=[jax.ShapeDtypeStruct((total_rows, n), BF)...  34.9 us
    ppermute x2, waiting for transfers between devices, per_device(): plus1 = [lax.ppermute(t, 'expert', up_ring) for t in own]  34.2 us
    all_to_all x5, starting transfers between devices, exchange(): lax.all_to_all(block, 'expert', 0, 0, tiled=True, axis_index_groups=PLANE...  25.4 us
    ppermute x2, waiting for transfers between devices, per_device(): plus2 = [lax.ppermute(t, 'expert', up_ring) for t in plus1]  23.5 us
    all_to_all x5, waiting for transfers between devices, exchange(): lax.all_to_all(block, 'expert', 0, 0, tiled=True, axis_index_groups=PLANE...  21.1 us
    pallas_call x4, Pallas kernels, pick_call(): pl.pallas_call(inner, grid=(width // TILE,), out_shape=[jax.ShapeDtypeStr...  18.8 us
    ppermute x1, waiting for transfers between devices, per_device(): plus3 = lax.ppermute(onward_up, 'expert', up_ring)  16.2 us
  transfers between devices with their start and end apart: 22, of which 13 were waited for; matrix products, arithmetic and copies ran while one was open for 1% of the time, Pallas kernels for 22%

profile of v1, /device:TPU:2, one launch (start us, length us, event | category | flops | bytes accessed | tf_op | source)
XLA Modules:
  0.0 380.2 jit_solution(6913122302056399584)
XLA Ops:
  12.5 24.9 %collective-permute-done.refs_0_.refs_2_ = bf16[272,2048]{1,0:T(8,128)(2,1)} collective-permute-done((bf16[272,2048]{1,0:T(8,128)(2,1)}, bf16[272,2048]{1,0:T(8,128)(2,1)}, u32[]{:S(2)}, u32[]{:S(2)}) %collective-permute-start) | collective-permute-done | bytes 1114144 | tf_op jit(solution)/shard_map/ppermute | solution.py:385
  59.1 12.3 %all-to-all-done = bf16[4,64,2048]{2,1,0:T(8,128)(2,1)} async-done(((bf16[4,64,2048]{2,1,0:T(8,128)(2,1)}), bf16[4,64,2048]{2,1,0:T(8,128)(2,1)}, u32[]{:S(2)}, u32[]{:S(2)}) %all-to-all-start) | async-done | bytes 1048608 | tf_op jit(solution)/shard_map/all_to_all | solution.py:391
  71.4 6.3 %shard_map.130 = (bf16[1024,2048]{1,0:T(8,128)(2,1)}, bf16[1024,2048]{1,0:T(8,128)(2,1)}, bf16[1024,384]{1,0:T(8,128)(2,1)}, bf16[1024,768]{1,0:T(8,128)(2,1)}, bf16[1024,2176]{1,0:T(8,128)(2,1)}) custom-call(s32[4]{0:T(128)} %pad_add_fusion.2.refs_0_, bf16[256,2048]{1,0:T(8,128)(2,1)} %bitcast.17.refs_1_, bf16[2048,384]{1,0:T(8,128)(2,1)} %bitcast.66, ...), custom_call_target="tpu_custom_call" | custom-call | flops 1 | bytes 1 | tf_op jit(solution)/shard_map/pallas_call | solution.py:293
  77.7 9.4 %collective-permute-done.4.refs_4_ = bf16[256,2048]{1,0:T(8,128)(2,1)} collective-permute-done((bf16[256,2048]{1,0:T(8,128)(2,1)}, bf16[256,2048]{1,0:T(8,128)(2,1)}, u32[]{:S(2)}, u32[]{:S(2)}) %collective-permute-start.4) | collective-permute-done | bytes 1048608 | tf_op jit(solution)/shard_map/ppermute | solution.py:385
  91.9 5.0 %all-to-all-start.1 = ((bf16[4,128,2048]{2,1,0:T(8,128)(2,1)}), bf16[4,128,2048]{2,1,0:T(8,128)(2,1)}, u32[]{:S(2)}, u32[]{:S(2)}) async-start(bf16[4,128,2048]{2,1,0:T(8,128)(2,1)} %bitcast.82), calls=%async_computation.1 | async-start | bytes 4194304 | tf_op jit(solution)/shard_map/all_to_all | solution.py:391
  100.2 23.5 %collective-permute-done.5.refs_4_ = bf16[256,2048]{1,0:T(8,128)(2,1)} collective-permute-done((bf16[256,2048]{1,0:T(8,128)(2,1)}, bf16[256,2048]{1,0:T(8,128)(2,1)}, u32[]{:S(2)}, u32[]{:S(2)}) %collective-permute-start.5) | collective-permute-done | bytes 1048608 | tf_op jit(solution)/shard_map/ppermute | solution.py:387
  123.7 5.0 %shard_map.132 = (bf16[384,2048]{1,0:T(8,128)(2,1)}, bf16[384,2048]{1,0:T(8,128)(2,1)}) custom-call(bf16[272,2048]{1,0:T(8,128)(2,1)} %collective-permute-done.1.refs_7_.refs_0_.refs_2_, bf16[272,2048]{1,0:T(8,128)(2,1)} %collective-permute-done.3.refs_8_.refs_1_.refs_3_, bf16[272,2048]{1,0:T(8,128)(2,1)} %collective-permute-done.1.refs_7_.refs_0_.refs_2_, ...), custom_call_target="tpu_custom_call" | custom-call | flops 1 | bytes 1 | tf_op jit(solution)/shard_map/pallas_call | solution.py:109
  142.2 7.4 %shard_map.134 = (bf16[1024,2048]{1,0:T(8,128)(2,1)}, bf16[1024,2048]{1,0:T(8,128)(2,1)}, bf16[1024,384]{1,0:T(8,128)(2,1)}, bf16[1024,768]{1,0:T(8,128)(2,1)}, bf16[1024,2176]{1,0:T(8,128)(2,1)}) custom-call(s32[8]{0:T(128)} %stack.154.refs_0_, ...), custom_call_target="tpu_custom_call", output_to_operand_aliasing={{0}: (6, {}), {1}: (7, {}), {2}: (8, {}), {3}: (9, {}), {4}... | custom-call | flops 1 | bytes 1 | tf_op jit(solution)/shard_map/pallas_call | solution.py:293
  149.7 16.2 %collective-permute-done.9.up_ref = bf16[384,2048]{1,0:T(8,128)(2,1)} collective-permute-done((bf16[384,2048]{1,0:T(8,128)(2,1)}, bf16[384,2048]{1,0:T(8,128)(2,1)}, u32[]{:S(2)}, u32[]{:S(2)}) %collective-permute-start.9) | collective-permute-done | bytes 1572896 | tf_op jit(solution)/shard_map/ppermute | solution.py:424
  170.7 5.0 %all-to-all-start.4 = ((bf16[4,128,2048]{2,1,0:T(8,128)(2,1)}), bf16[4,128,2048]{2,1,0:T(8,128)(2,1)}, u32[]{:S(2)}, u32[]{:S(2)}) async-start(bf16[4,128,2048]{2,1,0:T(8,128)(2,1)} %bitcast.84), calls=%async_computation.4 | async-start | bytes 4194304 | tf_op jit(solution)/shard_map/all_to_all | solution.py:391
  179.6 7.4 %shard_map.136 = (bf16[1024,2048]{1,0:T(8,128)(2,1)}, bf16[1024,2048]{1,0:T(8,128)(2,1)}, bf16[1024,384]{1,0:T(8,128)(2,1)}, bf16[1024,768]{1,0:T(8,128)(2,1)}, bf16[1024,2176]{1,0:T(8,128)(2,1)}) custom-call(s32[8]{0:T(128)} %stack.163.refs_0_, ...), custom_call_target="tpu_custom_call", output_to_operand_aliasing={{0}: (6, {}), {1}: (7, {}), {2}: (8, {}), {3}: (9, {}), {4}... | custom-call | flops 1 | bytes 1 | tf_op jit(solution)/shard_map/pallas_call | solution.py:293
  199.9 5.9 %all-to-all-start.3 = ((bf16[4,64,2048]{2,1,0:T(8,128)(2,1)}), bf16[4,64,2048]{2,1,0:T(8,128)(2,1)}, u32[]{:S(2)}, u32[]{:S(2)}) async-start(bf16[4,64,2048]{2,1,0:T(8,128)(2,1)} %bitcast.83), calls=%async_computation.3 | async-start | bytes 2097152 | tf_op jit(solution)/shard_map/all_to_all | solution.py:391
  207.1 7.4 %shard_map.138 = (bf16[1024,2048]{1,0:T(8,128)(2,1)}, bf16[1024,2048]{1,0:T(8,128)(2,1)}, bf16[1024,384]{1,0:T(8,128)(2,1)}, bf16[1024,768]{1,0:T(8,128)(2,1)}, bf16[1024,2176]{1,0:T(8,128)(2,1)}) custom-call(s32[8]{0:T(128)} %stack.172.refs_0_, ...), custom_call_target="tpu_custom_call", output_to_operand_aliasing={{0}: (6, {}), {1}: (7, {}), {2}: (8, {}), {3}: (9, {}), {4}... | custom-call | flops 1 | bytes 1 | tf_op jit(solution)/shard_map/pallas_call | solution.py:293
  218.7 6.4 %shard_map.139 = (bf16[1024,2048]{1,0:T(8,128)(2,1)}, bf16[1024,2048]{1,0:T(8,128)(2,1)}, bf16[1024,384]{1,0:T(8,128)(2,1)}, bf16[1024,768]{1,0:T(8,128)(2,1)}, bf16[1024,2176]{1,0:T(8,128)(2,1)}) custom-call(s32[4]{0:T(128)} %pad_add_fusion.1.refs_0_, ...), custom_call_target="tpu_custom_call", output_to_operand_aliasing={{0}: (5, {}), {1}: (6, {}), {2}: (7, {}), {3}: (8, {}), {4}... | custom-call | flops 1 | bytes 1 | tf_op jit(solution)/shard_map/pallas_call | solution.py:293
  225.1 5.1 %all-to-all-start.5 = ((bf16[16,64,2176]{2,1,0:T(8,128)(2,1)}), bf16[16,64,2176]{2,1,0:T(8,128)(2,1)}, u32[]{:S(2)}, u32[]{:S(2)}) async-start(bf16[16,64,2176]{2,1,0:T(8,128)(2,1)} %bitcast.65), calls=%async_computation.5 | async-start | bytes 8912896 | tf_op jit(solution)/shard_map/all_to_all | solution.py:448
  230.2 5.5 %shard_map.142.refs_0_.a_ref = bf16[384,2048]{1,0:T(8,128)(2,1)} custom-call(bf16[1024,384]{1,0:T(8,128)(2,1)} %get-tuple-element.65.left_ref, bf16[1024,2048]{1,0:T(8,128)(2,1)} %get-tuple-element.66.right_ref), custom_call_target="tpu_custom_call" | custom-call | flops 1 | bytes 1 | tf_op jit(solution)/shard_map/pallas_call | solution.py:329
  235.7 7.3 %shard_map.143.a_ref = bf16[2048,768]{1,0:T(8,128)(2,1)} custom-call(bf16[1024,2048]{1,0:T(8,128)(2,1)} %get-tuple-element.63.left_ref, bf16[1024,768]{1,0:T(8,128)(2,1)} %get-tuple-element.64.right_ref, bf16[384,2048]{1,0:T(8,128)(2,1)} %shard_map.142.refs_0_.a_ref), custom_call_target="tpu_custom_call" | custom-call | flops 1 | bytes 1 | tf_op jit(solution)/shard_map/pallas_call | solution.py:329
  243.0 4.9 %collective-permute-start.14 = (bf16[2048,768]{1,0:T(8,128)(2,1)}, bf16[2048,768]{1,0:T(8,128)(2,1)}, u32[]{:S(2)}, u32[]{:S(2)}) collective-permute-start(bf16[2048,768]{1,0:T(8,128)(2,1)} %shard_map.143.a_ref), channel_id=1, source_target_pairs={{0,224},{32,192},{64,160},{96,128},{128,96},{160,64},{192,32},{224... | collective-permute-start | bytes 9437192 | tf_op jit(solution)/shard_map/ppermute | solution.py:446
  249.3 80.8 %all-to-all-done.5 = bf16[16,64,2176]{2,1,0:T(8,128)(2,1)} async-done(((bf16[16,64,2176]{2,1,0:T(8,128)(2,1)}), bf16[16,64,2176]{2,1,0:T(8,128)(2,1)}, u32[]{:S(2)}, u32[]{:S(2)}) %all-to-all-start.5) | async-done | bytes 4456480 | tf_op jit(solution)/shard_map/all_to_all | solution.py:448
  330.1 5.0 %shard_map.141.refs_0_ = bf16[256,2176]{1,0:T(8,128)(2,1)} custom-call(s32[2]{0:T(128)} %pad_add_fusion.3.info_ref, s32[256,2]{1,0:T(8,128)} %copy-done.2, bf16[1024,2176]{1,0:T(8,128)(2,1)} %bitcast.54.back_ref), custom_call_target="tpu_custom_call" | custom-call | flops 1 | bytes 1 | tf_op jit(solution)/shard_map/pallas_call | solution.py:205
  337.4 4.9 %shard_map.140 = bf16[256,2176]{1,0:T(8,128)(2,1)} custom-call(s32[2]{0:T(128)} %pad_add_fusion.info_ref, s32[256,2]{1,0:T(8,128)} %copy-done.3, bf16[1024,2176]{1,0:T(8,128)(2,1)} %bitcast.54.back_ref), custom_call_target="tpu_custom_call" | custom-call | flops 1 | bytes 1 | tf_op jit(solution)/shard_map/pallas_call | solution.py:205
  342.3 9.3 %collective-permute-done.15.b_ref = bf16[384,2048]{1,0:T(8,128)(2,1)} collective-permute-done((bf16[384,2048]{1,0:T(8,128)(2,1)}, bf16[384,2048]{1,0:T(8,128)(2,1)}, u32[]{:S(2)}, u32[]{:S(2)}) %collective-permute-start.15) | collective-permute-done | bytes 1572896 | tf_op jit(solution)/shard_map/ppermute | solution.py:445
  355.6 5.0 %shard_map.145 = (bf16[2048,384]{1,0:T(8,128)(2,1)}, bf16[2048,384]{1,0:T(8,128)(2,1)}) custom-call(bf16[2048,768]{1,0:T(8,128)(2,1)} %shard_map.143.a_ref, bf16[2048,768]{1,0:T(8,128)(2,1)} %collective-permute-done.14.b_ref, bf16[384,2048]{1,0:T(8,128)(2,1)} %shard_map.144.refs_0_), custom_call_target="tpu_custom_call" | custom-call | flops 1 | bytes 1 | tf_op jit(solution)/shard_map/pallas_call | solution.py:355
  360.6 15.9 %collective-permute-done.13 = bf16[256,2176]{1,0:T(8,128)(2,1)} collective-permute-done((bf16[256,2176]{1,0:T(8,128)(2,1)}, bf16[256,2176]{1,0:T(8,128)(2,1)}, u32[]{:S(2)}, u32[]{:S(2)}) %collective-permute-start.13) | collective-permute-done | bytes 1114144 | tf_op jit(solution)/shard_map/ppermute | solution.py:457
  (65 shorter events, 93.7 us)
Async XLA Ops:
  0.6 43.2 %copy-start.5 = (s32[1,256,2]{1,2,0:T(2,128)S(1)}, s32[1,256,2]{1,2,0:T(2,128)}, u32[]{:S(2)}) copy-start(s32[1,256,2]{1,2,0:T(2,128)} %param.12) | copy-start | bytes 6148
  6.6 30.7 %collective-permute-start = (bf16[272,2048]{1,0:T(8,128)(2,1)}, bf16[272,2048]{1,0:T(8,128)(2,1)}, u32[]{:S(2)}, u32[]{:S(2)}) collective-permute-start(bf16[272,2048]{1,0:T(8,128)(2,1)} %shard_map.128.refs_0_.refs_1_), channel_id=1, source_target_pairs={{0,4},{1,5},{2,6},{3,7},{4,8},{5,9},{6,10},{7,11},{8,12},{9,13},{1... | collective-permute-start | bytes 3342344 | tf_op jit(solution)/shard_map/ppermute | solution.py:385
  8.5 28.8 %collective-permute-start.2 = (bf16[272,2048]{1,0:T(8,128)(2,1)}, bf16[272,2048]{1,0:T(8,128)(2,1)}, u32[]{:S(2)}, u32[]{:S(2)}) collective-permute-start(bf16[272,2048]{1,0:T(8,128)(2,1)} %shard_map.128.refs_0_.refs_1_), channel_id=1, source_target_pairs={{0,28},{1,29},{2,30},{3,31},{4,0},{5,1},{6,2},{7,3},{8,4},{9,5},{1... | collective-permute-start | bytes 3342344 | tf_op jit(solution)/shard_map/ppermute | solution.py:386
  37.3 49.8 %collective-permute-start.1 = (bf16[272,2048]{1,0:T(8,128)(2,1)}, bf16[272,2048]{1,0:T(8,128)(2,1)}, u32[]{:S(2)}, u32[]{:S(2)}) collective-permute-start(bf16[272,2048]{1,0:T(8,128)(2,1)} %collective-permute-done.refs_0_.refs_2_), channel_id=1, source_target_pairs={{0,4},{1,5},{2,6},{3,7},{4,8},{5,9},{6,10},{7,11},{8,12},{9,13},{1... | collective-permute-start | bytes 3342344 | tf_op jit(solution)/shard_map/ppermute | solution.py:387
  37.3 49.8 %collective-permute-start.3 = (bf16[272,2048]{1,0:T(8,128)(2,1)}, bf16[272,2048]{1,0:T(8,128)(2,1)}, u32[]{:S(2)}, u32[]{:S(2)}) collective-permute-start(bf16[272,2048]{1,0:T(8,128)(2,1)} %collective-permute-done.2.refs_1_.refs_3_), channel_id=1, source_target_pairs={{0,28},{1,29},{2,30},{3,31},{4,0},{5,1},{6,2},{7,3},{8,4},{9,5},{1... | collective-permute-start | bytes 3342344 | tf_op jit(solution)/shard_map/ppermute | solution.py:388
  40.6 46.5 %collective-permute-start.4 = (bf16[256,2048]{1,0:T(8,128)(2,1)}, bf16[256,2048]{1,0:T(8,128)(2,1)}, u32[]{:S(2)}, u32[]{:S(2)}) collective-permute-start(bf16[256,2048]{1,0:T(8,128)(2,1)} %bitcast.88), channel_id=1, source_target_pairs={{0,4},{1,5},{2,6},{3,7},{4,8},{5,9},{6,10},{7,11},{8,12},{9,13},{1... | collective-permute-start | bytes 3145736 | tf_op jit(solution)/shard_map/ppermute | solution.py:385
  40.6 46.5 %collective-permute-start.6 = (bf16[256,2048]{1,0:T(8,128)(2,1)}, bf16[256,2048]{1,0:T(8,128)(2,1)}, u32[]{:S(2)}, u32[]{:S(2)}) collective-permute-start(bf16[256,2048]{1,0:T(8,128)(2,1)} %bitcast.89), channel_id=1, source_target_pairs={{0,28},{1,29},{2,30},{3,31},{4,0},{5,1},{6,2},{7,3},{8,4},{9,5},{1... | collective-permute-start | bytes 3145736 | tf_op jit(solution)/shard_map/ppermute | solution.py:386
  44.0 48.0 %copy-start.3 = (s32[256,2]{1,0:T(8,128)}, s32[256,2]{1,0:T(8,128)S(1)}, u32[]{:S(2)}) copy-start(s32[256,2]{1,0:T(8,128)S(1)} %bitcast_add_fusion.place_ref) | copy-start | bytes 6148
  44.0 5.1 %collective-permute-start.8 = (s32[256,2]{1,0:T(8,128)S(1)}, s32[256,2]{1,0:T(8,128)S(1)}, u32[]{:S(2)}, u32[]{:S(2)}) collective-permute-start(s32[256,2]{1,0:T(8,128)S(1)} %bitcast_add_fusion.place_ref), channel_id=1, source_target_pairs={{0,2},{1,3},{2,0},{3,1},{4,6},{5,7},{6,4},{7,5},{8,10},{9,11},{10,... | collective-permute-start | bytes 6152 | tf_op jit(solution)/shard_map/ppermute | solution.py:382
  53.7 17.6 %all-to-all-start = ((bf16[4,64,2048]{2,1,0:T(8,128)(2,1)}), bf16[4,64,2048]{2,1,0:T(8,128)(2,1)}, u32[]{:S(2)}, u32[]{:S(2)}) async-start(bf16[4,64,2048]{2,1,0:T(8,128)(2,1)} %bitcast.86), calls=%async_computation | async-start | bytes 2097152 | tf_op jit(solution)/shard_map/all_to_all | solution.py:391
  91.9 44.9 %all-to-all-start.1 = ((bf16[4,128,2048]{2,1,0:T(8,128)(2,1)}), bf16[4,128,2048]{2,1,0:T(8,128)(2,1)}, u32[]{:S(2)}, u32[]{:S(2)}) async-start(bf16[4,128,2048]{2,1,0:T(8,128)(2,1)} %bitcast.82), calls=%async_computation.1 | async-start | bytes 4194304 | tf_op jit(solution)/shard_map/all_to_all | solution.py:391
  96.9 26.7 %collective-permute-start.5 = (bf16[256,2048]{1,0:T(8,128)(2,1)}, bf16[256,2048]{1,0:T(8,128)(2,1)}, u32[]{:S(2)}, u32[]{:S(2)}) collective-permute-start(bf16[256,2048]{1,0:T(8,128)(2,1)} %collective-permute-done.4.refs_4_), channel_id=1, source_target_pairs={{0,4},{1,5},{2,6},{3,7},{4,8},{5,9},{6,10},{7,11},{8,12},{9,13},{1... | collective-permute-start | bytes 3145736 | tf_op jit(solution)/shard_map/ppermute | solution.py:387
  96.9 26.7 %collective-permute-start.7 = (bf16[256,2048]{1,0:T(8,128)(2,1)}, bf16[256,2048]{1,0:T(8,128)(2,1)}, u32[]{:S(2)}, u32[]{:S(2)}) collective-permute-start(bf16[256,2048]{1,0:T(8,128)(2,1)} %collective-permute-done.6.refs_5_), channel_id=1, source_target_pairs={{0,28},{1,29},{2,30},{3,31},{4,0},{5,1},{6,2},{7,3},{8,4},{9,5},{1... | collective-permute-start | bytes 3145736 | tf_op jit(solution)/shard_map/ppermute | solution.py:388
  128.7 37.1 %collective-permute-start.9 = (bf16[384,2048]{1,0:T(8,128)(2,1)}, bf16[384,2048]{1,0:T(8,128)(2,1)}, u32[]{:S(2)}, u32[]{:S(2)}) collective-permute-start(bf16[384,2048]{1,0:T(8,128)(2,1)} %get-tuple-element.38.refs_6_), channel_id=1, source_target_pairs={{0,4},{1,5},{2,6},{3,7},{4,8},{5,9},{6,10},{7,11},{8,12},{9,13},{1... | collective-permute-start | bytes 4718600 | tf_op jit(solution)/shard_map/ppermute | solution.py:424
  130.8 35.7 %collective-permute-start.10 = (bf16[384,2048]{1,0:T(8,128)(2,1)}, bf16[384,2048]{1,0:T(8,128)(2,1)}, u32[]{:S(2)}, u32[]{:S(2)}) collective-permute-start(bf16[384,2048]{1,0:T(8,128)(2,1)} %get-tuple-element.39), channel_id=1, source_target_pairs={{0,28},{1,29},{2,30},{3,31},{4,0},{5,1},{6,2},{7,3},{8,4},{9,5},{1... | collective-permute-start | bytes 4718600 | tf_op jit(solution)/shard_map/ppermute | solution.py:425
  136.8 33.9 %all-to-all-start.2 = ((bf16[4,128,2048]{2,1,0:T(8,128)(2,1)}), bf16[4,128,2048]{2,1,0:T(8,128)(2,1)}, u32[]{:S(2)}, u32[]{:S(2)}) async-start(bf16[4,128,2048]{2,1,0:T(8,128)(2,1)} %bitcast.81), calls=%async_computation.2 | async-start | bytes 4194304 | tf_op jit(solution)/shard_map/all_to_all | solution.py:391
  170.7 29.2 %all-to-all-start.4 = ((bf16[4,128,2048]{2,1,0:T(8,128)(2,1)}), bf16[4,128,2048]{2,1,0:T(8,128)(2,1)}, u32[]{:S(2)}, u32[]{:S(2)}) async-start(bf16[4,128,2048]{2,1,0:T(8,128)(2,1)} %bitcast.84), calls=%async_computation.4 | async-start | bytes 4194304 | tf_op jit(solution)/shard_map/all_to_all | solution.py:391
  175.7 15.4 %collective-permute-start.11 = (bf16[128,2048]{1,0:T(8,128)(2,1)}, bf16[128,2048]{1,0:T(8,128)(2,1)S(1)}, u32[]{:S(2)}, u32[]{:S(2)}) collective-permute-start(bf16[128,2048]{1,0:T(8,128)(2,1)} %get-tuple-element.45), channel_id=1, source_target_pairs={{0,4},{1,5},{2,6},{3,7},{4,8},{5,9},{6,10},{7,11},{8,12},{9,13},{1... | collective-permute-start | bytes 1572872 | tf_op jit(solution)/shard_map/ppermute | solution.py:432
  177.2 14.0 %collective-permute-start.12 = (bf16[128,2048]{1,0:T(8,128)(2,1)}, bf16[128,2048]{1,0:T(8,128)(2,1)}, u32[]{:S(2)}, u32[]{:S(2)}) collective-permute-start(bf16[128,2048]{1,0:T(8,128)(2,1)} %get-tuple-element.46), channel_id=1, source_target_pairs={{0,28},{1,29},{2,30},{3,31},{4,0},{5,1},{6,2},{7,3},{8,4},{9,5},{1... | collective-permute-start | bytes 1572872 | tf_op jit(solution)/shard_map/ppermute | solution.py:433
  199.9 18.8 %all-to-all-start.3 = ((bf16[4,64,2048]{2,1,0:T(8,128)(2,1)}), bf16[4,64,2048]{2,1,0:T(8,128)(2,1)}, u32[]{:S(2)}, u32[]{:S(2)}) async-start(bf16[4,64,2048]{2,1,0:T(8,128)(2,1)} %bitcast.83), calls=%async_computation.3 | async-start | bytes 2097152 | tf_op jit(solution)/shard_map/all_to_all | solution.py:391
  225.1 105.0 %all-to-all-start.5 = ((bf16[16,64,2176]{2,1,0:T(8,128)(2,1)}), bf16[16,64,2176]{2,1,0:T(8,128)(2,1)}, u32[]{:S(2)}, u32[]{:S(2)}) async-start(bf16[16,64,2176]{2,1,0:T(8,128)(2,1)} %bitcast.65), calls=%async_computation.5 | async-start | bytes 8912896 | tf_op jit(solution)/shard_map/all_to_all | solution.py:448
  243.0 112.5 %collective-permute-start.14 = (bf16[2048,768]{1,0:T(8,128)(2,1)}, bf16[2048,768]{1,0:T(8,128)(2,1)}, u32[]{:S(2)}, u32[]{:S(2)}) collective-permute-start(bf16[2048,768]{1,0:T(8,128)(2,1)} %shard_map.143.a_ref), channel_id=1, source_target_pairs={{0,224},{32,192},{64,160},{96,128},{128,96},{160,64},{192,32},{224... | collective-permute-start | bytes 9437192 | tf_op jit(solution)/shard_map/ppermute | solution.py:446
  247.9 103.7 %collective-permute-start.15 = (bf16[384,2048]{1,0:T(8,128)(2,1)}, bf16[384,2048]{1,0:T(8,128)(2,1)}, u32[]{:S(2)}, u32[]{:S(2)}) collective-permute-start(bf16[384,2048]{1,0:T(8,128)(2,1)} %shard_map.142.refs_0_.a_ref), channel_id=1, source_target_pairs={{0,224},{32,192},{64,160},{96,128},{128,96},{160,64},{192,32},{224... | collective-permute-start | bytes 4718600 | tf_op jit(solution)/shard_map/ppermute | solution.py:445
  335.1 41.3 %collective-permute-start.13 = (bf16[256,2176]{1,0:T(8,128)(2,1)}, bf16[256,2176]{1,0:T(8,128)(2,1)}, u32[]{:S(2)}, u32[]{:S(2)}) collective-permute-start(bf16[256,2176]{1,0:T(8,128)(2,1)} %shard_map.141.refs_0_), channel_id=1, source_target_pairs={{0,2},{1,3},{2,0},{3,1},{4,6},{5,7},{6,4},{7,5},{8,10},{9,11},{10,... | collective-permute-start | bytes 3342344 | tf_op jit(solution)/shard_map/ppermute | solution.py:457
  (4 other events, 44.7 us)

commit v2 on v1

--- a/solution.py
+++ b/solution.py
@@ -41,91 +41,89 @@
 TILE = 512
 
 
-def route_rows(acts, source_row, expert_of, combine, me):
+def route_rows(acts, grads, source_row, experts_of, combine, me):
     tok, width = acts.shape
     most = source_row.shape[1]
     slots = LANES * most
-
-    def body(me_ref, acts_ref, source_ref, expert_ref, combine_ref, out_ref, table_ref):
+    behind = tok + ROUTE_ROWS
+
+    def body(me_ref, acts_ref, grads_ref, source_ref, expert_ref, combine_ref, out_ref, table):
         own = me_ref[0]
         own_z = own // LANES
         out_ref[:tok, :] = acts_ref[...]
-        names = lax.broadcasted_iota(jnp.int32, (tok, slots), 0)
+        out_ref[behind:, :] = grads_ref[...]
+        index = lax.broadcasted_iota(jnp.int32, (tok, slots), 0)
         which = lax.broadcasted_iota(jnp.int32, (1, slots), 1) // most
-        wide = combine_ref[...].astype(F32)
+        experts = expert_ref[...].astype(F32).astype(BF)
         for p in range(RING):
             plane = lax.rem(own_z + p, RING) * LANES
             for r in range(LANES):
                 row = source_ref[pl.ds(plane + r, 1), :]
                 row = jnp.where(row >= 0, row - own * tok, -1)
-                table_ref[p : p + 1, r * most : (r + 1) * most] = row.astype(F32)
-            hot = names == table_ref[p : p + 1, :].astype(jnp.int32)
-            expert = plane + which
-            weight = jnp.zeros((tok, slots), F32)
-            for k in range(2):
-                chosen = expert_ref[:, k : k + 1] == expert
-                weight = weight + jnp.where(chosen, wide[:, k : k + 1], 0.0)
-            weight = jnp.sum(jnp.where(hot, weight, 0.0), axis=0, keepdims=True)
-            table_ref[RING + p : RING + p + 1, :] = weight
-        out_ref[tok:, :] = jnp.zeros((ROUTE_ROWS, width), BF)
-        out_ref[tok:, :slots] = table_ref[...].astype(BF)
-
-    return pl.pallas_call(
-        body,
-        out_shape=jax.ShapeDtypeStruct((tok + ROUTE_ROWS, width), BF),
-        in_specs=[pl.BlockSpec(memory_space=pltpu.SMEM)] + [WHOLE] * 4,
+                table[p : p + 1, r * most : (r + 1) * most] = row.astype(F32)
+            hot = index == table[p : p + 1, :].astype(jnp.int32)
+            hot = hot.astype(F32).astype(BF)
+            named = dot(experts, hot)
+            value = dot(combine_ref[...], hot)
+            expert = (plane + which).astype(F32)
+            weight = jnp.where(named == expert, value, 0.0)
+            table[RING + p : RING + p + 1, :] = weight[0:1] + weight[1:2]
+        out_ref[tok:behind, :] = jnp.zeros((ROUTE_ROWS, width), BF)
+        out_ref[tok:behind, :slots] = table[...].astype(BF)
+
+    return pl.pallas_call(
+        body,
+        out_shape=jax.ShapeDtypeStruct((behind + tok, width), BF),
+        in_specs=[pl.BlockSpec(memory_space=pltpu.SMEM)] + [WHOLE] * 5,
         out_specs=WHOLE,
         scratch_shapes=[pltpu.VMEM((ROUTE_ROWS, slots), F32)],
         cost_estimate=LIGHT,
         compiler_params=PARAMS,
-    )(me.reshape(1), acts, source_row, expert_of, combine)
-
-
-def pick(route, plane, x_ref, g_ref):
-    tok = g_ref.shape[0]
+    )(me.reshape(1), acts, grads, source_row, experts_of, combine)
+
+
+def pick(route, plane, ref):
+    tok = (ref.shape[0] - ROUTE_ROWS) // 2
     names = route[plane : plane + 1, :].astype(jnp.int32)
     index = lax.broadcasted_iota(jnp.int32, (tok, names.shape[1]), 0)
     hot = index == names
     weight = jnp.where(hot, route[RING + plane : RING + plane + 1, :], 0.0).astype(BF)
-    x = dot(hot.astype(F32).astype(BF), x_ref[:tok, :], FIRST).astype(BF)
-    return x, dot(weight, g_ref[...], FIRST).astype(BF)
+    x = dot(hot.astype(F32).astype(BF), ref[:tok, :], FIRST).astype(BF)
+    return x, dot(weight, ref[tok + ROUTE_ROWS :, :], FIRST).astype(BF)
 
 
 def pick_call(body, sources, out_rows, after):
-    tok, width = sources[0][1].shape
+    rows, width = sources[0].shape
+    tok = (rows - ROUTE_ROWS) // 2
     count = len(sources)
     slots = LANES * 32
 
     def inner(*refs):
         routes = [r[:, :slots].astype(F32) for r in refs[:count]]
-        outs = refs[3 * count + len(after) :]
-        body(routes, refs[count : 2 * count], refs[2 * count : 3 * count], outs)
-
-    def columns(rows):
-        return pl.BlockSpec((rows, TILE), lambda i: (0, i))
-
-    xs = [x for x, _ in sources]
-    gs = [g for _, g in sources]
+        body(routes, refs[count : 2 * count], refs[2 * count + len(after) :])
+
+    def columns(size):
+        return pl.BlockSpec((size, TILE), lambda i: (0, i))
+
     return pl.pallas_call(
         inner,
         grid=(width // TILE,),
         out_shape=[jax.ShapeDtypeStruct((n, width), BF) for n in out_rows],
         in_specs=[pl.BlockSpec((ROUTE_ROWS, TILE), lambda i: (tok // ROUTE_ROWS, 0))] * count
-        + [columns(tok + ROUTE_ROWS)] * count
-        + [columns(tok)] * count
+        + [columns(rows)] * count
         + [ANYWHERE] * len(after),
         out_specs=[columns(n) for n in out_rows],
         cost_estimate=LIGHT,
         compiler_params=PARAMS,
-    )(*xs, *xs, *gs, *after)
+    )(*sources, *sources, *after)
 
 
 def pick_lanes(sources, planes, most, after=()):
     size = len(sources) * 2 * most
 
-    def body(routes, x_refs, g_refs, outs):
+    def body(routes, refs, outs):
         for i in range(len(sources)):
-            for t, rows in enumerate(pick(routes[i], planes[i], x_refs[i], g_refs[i])):
+            for t, rows in enumerate(pick(routes[i], planes[i], refs[i])):
                 for r in range(LANES):
                     at = r * size + (2 * i + t) * most
                     outs[0][at : at + most, :] = rows[r * most : (r + 1) * most]
@@ -137,13 +135,13 @@
     half = most // 2
     low = 2 * LANES * most
 
-    def body(routes, x_refs, g_refs, outs):
+    def body(routes, refs, outs):
         for d in range(2):
-            for t, rows in enumerate(pick(routes[d], planes[d][0], x_refs[d], g_refs[d])):
+            for t, rows in enumerate(pick(routes[d], planes[d][0], refs[d])):
                 for r in range(LANES):
                     to = (2 * r + t) * most
                     outs[d][to : to + most, :] = rows[r * most : (r + 1) * most]
-            for t, rows in enumerate(pick(routes[d], planes[d][1], x_refs[d], g_refs[d])):
+            for t, rows in enumerate(pick(routes[d], planes[d][1], refs[d])):
                 for r in range(LANES):
                     to, at = low + (2 * r + t) * half, r * most + d * half
                     outs[d][to : to + half, :] = rows[at : at + half]
@@ -313,13 +311,14 @@
     )(places, block, *weights, *after, *shared)
 
 
-def weight_grads(left, right, across, after=()):
-    count = left.shape[0]
-    shape = (left.shape[1], right.shape[1])
+def weight_grads(x, d, hidden, g):
+    count, width = x.shape
+    ff = hidden.shape[1]
     tile = 512
 
-    def body(left_ref, right_ref, *refs):
-        refs[-1][...] = dot(left_ref[...], right_ref[...], FIRST).astype(BF)
+    def body(x_ref, d_ref, hidden_ref, g_ref, down_ref, in_ref):
+        down_ref[...] = dot(hidden_ref[...], g_ref[...], FIRST).astype(BF)
+        in_ref[...] = dot(x_ref[...], d_ref[...], FIRST).astype(BF)
 
     def fixed(a):
         return pl.BlockSpec(a.shape, lambda i: (0, 0))
@@ -328,16 +327,19 @@
 
     return pl.pallas_call(
         body,
-        grid=(shape[1] // tile if across else shape[0] // tile,),
-        out_shape=jax.ShapeDtypeStruct(shape, BF),
-        in_specs=([fixed(left), moving] if across else [moving, fixed(right)])
-        + [ANYWHERE] * len(after),
-        out_specs=pl.BlockSpec((shape[0], tile), lambda i: (0, i))
-        if across
-        else pl.BlockSpec((tile, shape[1]), lambda i: (i, 0)),
-        cost_estimate=LIGHT,
-        compiler_params=PARAMS,
-    )(left, right, *after)
+        grid=(width // tile,),
+        out_shape=[
+            jax.ShapeDtypeStruct((ff, width), BF),
+            jax.ShapeDtypeStruct((width, 2 * ff), BF),
+        ],
+        in_specs=[moving, fixed(d), fixed(hidden), moving],
+        out_specs=[
+            pl.BlockSpec((ff, tile), lambda i: (0, i)),
+            pl.BlockSpec((tile, 2 * ff), lambda i: (i, 0)),
+        ],
+        cost_estimate=LIGHT,
+        compiler_params=PARAMS,
+    )(x, d, hidden, g)
 
 
 def total(a, b, parts, after):
@@ -380,12 +382,13 @@
 
     place = expert_of[0] * most + (slot_of[0] - me * most)
     place_across = lax.ppermute(place, "expert", ACROSS)
-    routed = route_rows(acts[0], source_row[0], expert_of[0], combine[0], me)
-    own = (routed, grad_out[0])
-    plus1 = [lax.ppermute(t, "expert", up_ring) for t in own]
-    minus1 = [lax.ppermute(t, "expert", down_ring) for t in own]
-    plus2 = [lax.ppermute(t, "expert", up_ring) for t in plus1]
-    minus2 = [lax.ppermute(t, "expert", down_ring) for t in minus1]
+    own = route_rows(
+        acts[0], grad_out[0], source_row[0], expert_of[0].T, combine[0].T, me
+    )
+    plus1 = lax.ppermute(own, "expert", up_ring)
+    minus1 = lax.ppermute(own, "expert", down_ring)
+    plus2 = lax.ppermute(plus1, "expert", up_ring)
+    minus2 = lax.ppermute(minus1, "expert", down_ring)
 
     def exchange(block):
         return lax.all_to_all(
@@ -414,12 +417,10 @@
     own_out = pick_lanes([own], [0], most, after=[place_across])
     here_rows = exchange(own_out)
     shared = work(0, here_rows, most, [])
-    near_out = pick_lanes(
-        [plus1, minus1], [1, RING - 1], most, after=[shared[4], plus2[0], minus2[0]]
-    )
+    near_out = pick_lanes([plus1, minus1], [1, RING - 1], most, after=[own_out])
     near = exchange(near_out)
     onward_up, onward_down = pick_onward(
-        [plus2, minus2], [[3, 4], [RING - 3, RING - 4]], most, after=[near_out]
+        [plus2, minus2], [[3, 4], [RING - 3, RING - 4]], most, after=[near_out, shared[4]]
     )
     plus3 = lax.ppermute(onward_up, "expert", up_ring)
     minus3 = lax.ppermute(onward_down, "expert", down_ring)
@@ -439,8 +440,7 @@
     shared = work(4, last, most // 2, shared)
 
     x_all, g_all, hidden, d_rows, dx = shared
-    down_part = weight_grads(hidden, g_all, True)
-    in_parts = weight_grads(x_all, d_rows, False, after=[down_part])
+    down_part, in_parts = weight_grads(x_all, d_rows, hidden, g_all)
     mirror = [(s, sections - 1 - s) for s in range(sections)]
     down_far = lax.ppermute(down_part, "section", mirror)
     in_far = lax.ppermute(in_parts, "section", mirror)

time: 382 us -> 362 us (0.948)
  waiting for transfers between devices: 210 us -> 201 us
  starting transfers between devices: 60.4 us -> 54.4 us
    all_to_all x5, waiting for transfers between devices: 21.1 us -> 8.78 us  [exchange(): lax.all_to_all(block, 'expert', 0, 0, tiled=True, axis_index_groups=PLANE...]
    ppermute x8 -> x4, starting transfers between devices: 15.6 us -> 9.1 us  [the longest x1 3.94 us: per_device(): minus1 = lax.ppermute(own, 'expert', down_ring)]
    ppermute x8 -> x4, waiting for transfers between devices: 57.7 us -> 62.4 us  [the longest x1 32.7 us: per_device(): plus1 = lax.ppermute(own, 'expert', up_ring)]
    pallas_call x3 -> x2, Pallas kernels: 15.9 us -> 12.8 us  [the longest x1 9.49 us: weight_grads(): pl.pallas_call(body, grid=(width // tile,), out_shape=[jax.ShapeDtypeStru...]
  transfers between devices with their start and end apart: 22 -> 18, of which waited for: 13 -> 11; matrix products, arithmetic and copies ran while one was open for 1% -> 1% of each run, Pallas kernels for 22% -> 23%
where the time goes in v2:
time: 362 us; the launch traced here: 360 us
  waiting for transfers between devices  201 us (56%)
  Pallas kernels  93 us (26%)
  starting transfers between devices  54.4 us (15%)
  local copies, waits for them, and re-layouts  6.02 us (2%)
  other arithmetic  5.07 us (1%)
    all_to_all x1, waiting for transfers between devices, per_device(): lax.all_to_all(dx.reshape(2 * RING, 2 * most, width + SCORE), 'expert', 0...  84.2 us
    pallas_call x5, Pallas kernels, chunk_grads(): pl.pallas_call(body, out_shape=[jax.ShapeDtypeStruct((total_rows, n), BF)...  34.9 us
    ppermute x1, waiting for transfers between devices, per_device(): plus1 = lax.ppermute(own, 'expert', up_ring)  32.7 us
    ppermute x1, waiting for transfers between devices, per_device(): plus2 = lax.ppermute(plus1, 'expert', up_ring)  29.7 us
    all_to_all x5, starting transfers between devices, exchange(): lax.all_to_all(block, 'expert', 0, 0, tiled=True, axis_index_groups=PLANE...  25.5 us
    pallas_call x4, Pallas kernels, pick_call(): pl.pallas_call(inner, grid=(width // TILE,), out_shape=[jax.ShapeDtypeStr...  18.8 us
    ppermute x1, waiting for transfers between devices, per_device(): away = lax.ppermute(leaving, 'expert', ACROSS)  15.8 us
    ppermute x1, waiting for transfers between devices, per_device(): plus3 = lax.ppermute(onward_up, 'expert', up_ring)  15 us
  transfers between devices with their start and end apart: 18, of which 11 were waited for; matrix products, arithmetic and copies ran while one was open for 1% of the time, Pallas kernels for 23%

profile of v2, /device:TPU:2, one launch (start us, length us, event | category | flops | bytes accessed | tf_op | source)
XLA Modules:
  0.0 360.2 jit_solution(17312885658101421724)
XLA Ops:
  25.9 32.7 %collective-permute-done.refs_0_.refs_2_ = bf16[528,2048]{1,0:T(8,128)(2,1)} collective-permute-done((bf16[528,2048]{1,0:T(8,128)(2,1)}, bf16[528,2048]{1,0:T(8,128)(2,1)}, u32[]{:S(2)}, u32[]{:S(2)}) %collective-permute-start) | collective-permute-done | bytes 2162720 | tf_op jit(solution)/shard_map/ppermute | solution.py:388
  61.8 4.8 %shard_map.130.refs_4_ = bf16[512,2048]{1,0:T(8,128)(2,1)} custom-call(bf16[528,2048]{1,0:T(8,128)(2,1)} %collective-permute-done.refs_0_.refs_2_, bf16[528,2048]{1,0:T(8,128)(2,1)} %collective-permute-done.2.refs_1_.refs_3_, bf16[528,2048]{1,0:T(8,128)(2,1)} %collective-permute-done.refs_0_.refs_2_, ...), custom_call_target="tpu_custom_call" | custom-call | flops 1 | bytes 1 | tf_op jit(solution)/shard_map/pallas_call | solution.py:108
  66.7 5.0 %all-to-all-start.1 = ((bf16[4,128,2048]{2,1,0:T(8,128)(2,1)}), bf16[4,128,2048]{2,1,0:T(8,128)(2,1)}, u32[]{:S(2)}, u32[]{:S(2)}) async-start(bf16[4,128,2048]{2,1,0:T(8,128)(2,1)} %bitcast.88), calls=%async_computation.1 | async-start | bytes 4194304 | tf_op jit(solution)/shard_map/all_to_all | solution.py:394
  72.2 6.4 %shard_map.131 = (bf16[1024,2048]{1,0:T(8,128)(2,1)}, bf16[1024,2048]{1,0:T(8,128)(2,1)}, bf16[1024,384]{1,0:T(8,128)(2,1)}, bf16[1024,768]{1,0:T(8,128)(2,1)}, bf16[1024,2176]{1,0:T(8,128)(2,1)}) custom-call(s32[4]{0:T(128)} %pad_add_fusion.2.refs_0_, bf16[256,2048]{1,0:T(8,128)(2,1)} %bitcast.19.refs_1_, bf16[2048,384]{1,0:T(8,128)(2,1)} %bitcast.72, ...), custom_call_target="tpu_custom_call" | custom-call | flops 1 | bytes 1 | tf_op jit(solution)/shard_map/pallas_call | solution.py:291
  78.6 29.7 %collective-permute-done.1.refs_0_.refs_2_ = bf16[528,2048]{1,0:T(8,128)(2,1)} collective-permute-done((bf16[528,2048]{1,0:T(8,128)(2,1)}, bf16[528,2048]{1,0:T(8,128)(2,1)}, u32[]{:S(2)}, u32[]{:S(2)}) %collective-permute-start.1) | collective-permute-done | bytes 2162720 | tf_op jit(solution)/shard_map/ppermute | solution.py:390
  108.4 5.1 %shard_map.132 = (bf16[384,2048]{1,0:T(8,128)(2,1)}, bf16[384,2048]{1,0:T(8,128)(2,1)}) custom-call(bf16[528,2048]{1,0:T(8,128)(2,1)} %collective-permute-done.1.refs_0_.refs_2_, bf16[528,2048]{1,0:T(8,128)(2,1)} %collective-permute-done.3.refs_1_.refs_3_, bf16[528,2048]{1,0:T(8,128)(2,1)} %collective-permute-done.1.refs_0_.refs_2_, ...), custom_call_target="tpu_custom_call" | custom-call | flops 1 | bytes 1 | tf_op jit(solution)/shard_map/pallas_call | solution.py:108
  116.7 4.9 %shard_map.133.refs_5_ = bf16[512,2048]{1,0:T(8,128)(2,1)} custom-call(bf16[528,2048]{1,0:T(8,128)(2,1)} %collective-permute-done.1.refs_0_.refs_2_, bf16[528,2048]{1,0:T(8,128)(2,1)} %collective-permute-done.3.refs_1_.refs_3_, bf16[528,2048]{1,0:T(8,128)(2,1)} %collective-permute-done.1.refs_0_.refs_2_, ...), custom_call_target="tpu_custom_call" | custom-call | flops 1 | bytes 1 | tf_op jit(solution)/shard_map/pallas_call | solution.py:108
  121.5 5.0 %all-to-all-start.2 = ((bf16[4,128,2048]{2,1,0:T(8,128)(2,1)}), bf16[4,128,2048]{2,1,0:T(8,128)(2,1)}, u32[]{:S(2)}, u32[]{:S(2)}) async-start(bf16[4,128,2048]{2,1,0:T(8,128)(2,1)} %bitcast.87), calls=%async_computation.2 | async-start | bytes 4194304 | tf_op jit(solution)/shard_map/all_to_all | solution.py:394
  127.2 7.4 %shard_map.134 = (bf16[1024,2048]{1,0:T(8,128)(2,1)}, bf16[1024,2048]{1,0:T(8,128)(2,1)}, bf16[1024,384]{1,0:T(8,128)(2,1)}, bf16[1024,768]{1,0:T(8,128)(2,1)}, bf16[1024,2176]{1,0:T(8,128)(2,1)}) custom-call(s32[8]{0:T(128)} %stack.154.refs_0_, ...), custom_call_target="tpu_custom_call", output_to_operand_aliasing={{0}: (6, {}), {1}: (7, {}), {2}: (8, {}), {3}: (9, {}), {4}... | custom-call | flops 1 | bytes 1 | tf_op jit(solution)/shard_map/pallas_call | solution.py:291
  134.6 15.0 %collective-permute-done.5.up_ref = bf16[384,2048]{1,0:T(8,128)(2,1)} collective-permute-done((bf16[384,2048]{1,0:T(8,128)(2,1)}, bf16[384,2048]{1,0:T(8,128)(2,1)}, u32[]{:S(2)}, u32[]{:S(2)}) %collective-permute-start.5) | collective-permute-done | bytes 1572896 | tf_op jit(solution)/shard_map/ppermute | solution.py:425
  153.9 5.0 %all-to-all-start.4 = ((bf16[4,128,2048]{2,1,0:T(8,128)(2,1)}), bf16[4,128,2048]{2,1,0:T(8,128)(2,1)}, u32[]{:S(2)}, u32[]{:S(2)}) async-start(bf16[4,128,2048]{2,1,0:T(8,128)(2,1)} %bitcast.91), calls=%async_computation.4 | async-start | bytes 4194304 | tf_op jit(solution)/shard_map/all_to_all | solution.py:394
  162.7 7.4 %shard_map.136 = (bf16[1024,2048]{1,0:T(8,128)(2,1)}, bf16[1024,2048]{1,0:T(8,128)(2,1)}, bf16[1024,384]{1,0:T(8,128)(2,1)}, bf16[1024,768]{1,0:T(8,128)(2,1)}, bf16[1024,2176]{1,0:T(8,128)(2,1)}) custom-call(s32[8]{0:T(128)} %stack.163.refs_0_, ...), custom_call_target="tpu_custom_call", output_to_operand_aliasing={{0}: (6, {}), {1}: (7, {}), {2}: (8, {}), {3}: (9, {}), {4}... | custom-call | flops 1 | bytes 1 | tf_op jit(solution)/shard_map/pallas_call | solution.py:291
  183.0 5.9 %all-to-all-start.3 = ((bf16[4,64,2048]{2,1,0:T(8,128)(2,1)}), bf16[4,64,2048]{2,1,0:T(8,128)(2,1)}, u32[]{:S(2)}, u32[]{:S(2)}) async-start(bf16[4,64,2048]{2,1,0:T(8,128)(2,1)} %bitcast.89), calls=%async_computation.3 | async-start | bytes 2097152 | tf_op jit(solution)/shard_map/all_to_all | solution.py:394
  190.2 7.4 %shard_map.138 = (bf16[1024,2048]{1,0:T(8,128)(2,1)}, bf16[1024,2048]{1,0:T(8,128)(2,1)}, bf16[1024,384]{1,0:T(8,128)(2,1)}, bf16[1024,768]{1,0:T(8,128)(2,1)}, bf16[1024,2176]{1,0:T(8,128)(2,1)}) custom-call(s32[8]{0:T(128)} %stack.172.refs_0_, ...), custom_call_target="tpu_custom_call", output_to_operand_aliasing={{0}: (6, {}), {1}: (7, {}), {2}: (8, {}), {3}: (9, {}), {4}... | custom-call | flops 1 | bytes 1 | tf_op jit(solution)/shard_map/pallas_call | solution.py:291
  201.8 6.4 %shard_map.139 = (bf16[1024,2048]{1,0:T(8,128)(2,1)}, bf16[1024,2048]{1,0:T(8,128)(2,1)}, bf16[1024,384]{1,0:T(8,128)(2,1)}, bf16[1024,768]{1,0:T(8,128)(2,1)}, bf16[1024,2176]{1,0:T(8,128)(2,1)}) custom-call(s32[4]{0:T(128)} %pad_add_fusion.1.refs_0_, ...), custom_call_target="tpu_custom_call", output_to_operand_aliasing={{0}: (5, {}), {1}: (6, {}), {2}: (7, {}), {3}: (8, {}), {4}... | custom-call | flops 1 | bytes 1 | tf_op jit(solution)/shard_map/pallas_call | solution.py:291
  208.2 5.4 %all-to-all-start.5 = ((bf16[16,64,2176]{2,1,0:T(8,128)(2,1)}), bf16[16,64,2176]{2,1,0:T(8,128)(2,1)}, u32[]{:S(2)}, u32[]{:S(2)}) async-start(bf16[16,64,2176]{2,1,0:T(8,128)(2,1)} %bitcast.71), calls=%async_computation.5 | async-start | bytes 8912896 | tf_op jit(solution)/shard_map/all_to_all | solution.py:448
  213.6 9.5 %shard_map.142 = (bf16[384,2048]{1,0:T(8,128)(2,1)}, bf16[2048,768]{1,0:T(8,128)(2,1)}) custom-call(bf16[1024,2048]{1,0:T(8,128)(2,1)} %get-tuple-element.65.x_ref, bf16[1024,768]{1,0:T(8,128)(2,1)} %get-tuple-element.66.d_ref, bf16[1024,384]{1,0:T(8,128)(2,1)} %get-tuple-element.67.hidden_ref, bf16[1024,2048]{1,0:T(8,128)(2,1)} %get-tuple-element.68.g_ref), custom_call_target="tpu_custom_call" | custom-call | flops 1 | bytes 1 | tf_op jit(solution)/shard_map/pallas_call | solution.py:328
  223.1 4.8 %collective-permute-start.10 = (bf16[2048,768]{1,0:T(8,128)(2,1)}, bf16[2048,768]{1,0:T(8,128)(2,1)}, u32[]{:S(2)}, u32[]{:S(2)}) collective-permute-start(bf16[2048,768]{1,0:T(8,128)(2,1)} %get-tuple-element.69.a_ref), channel_id=1, source_target_pairs={{0,224},{32,192},{64,160},{96,128},{128,96},{160,64},{192,32},{224... | collective-permute-start | bytes 9437192 | tf_op jit(solution)/shard_map/ppermute | solution.py:446
  229.3 84.2 %all-to-all-done.5 = bf16[16,64,2176]{2,1,0:T(8,128)(2,1)} async-done(((bf16[16,64,2176]{2,1,0:T(8,128)(2,1)}), bf16[16,64,2176]{2,1,0:T(8,128)(2,1)}, u32[]{:S(2)}, u32[]{:S(2)}) %all-to-all-start.5) | async-done | bytes 4456480 | tf_op jit(solution)/shard_map/all_to_all | solution.py:448
  313.5 5.0 %shard_map.141.refs_0_ = bf16[256,2176]{1,0:T(8,128)(2,1)} custom-call(s32[2]{0:T(128)} %pad_add_fusion.3.info_ref, s32[256,2]{1,0:T(8,128)} %copy-done.1, bf16[1024,2176]{1,0:T(8,128)(2,1)} %bitcast.56.back_ref), custom_call_target="tpu_custom_call" | custom-call | flops 1 | bytes 1 | tf_op jit(solution)/shard_map/pallas_call | solution.py:203
  320.7 4.9 %shard_map.140 = bf16[256,2176]{1,0:T(8,128)(2,1)} custom-call(s32[2]{0:T(128)} %pad_add_fusion.info_ref, s32[256,2]{1,0:T(8,128)} %copy-done.2, bf16[1024,2176]{1,0:T(8,128)(2,1)} %bitcast.56.back_ref), custom_call_target="tpu_custom_call" | custom-call | flops 1 | bytes 1 | tf_op jit(solution)/shard_map/pallas_call | solution.py:203
  325.7 6.0 %collective-permute-done.11.b_ref = bf16[384,2048]{1,0:T(8,128)(2,1)} collective-permute-done((bf16[384,2048]{1,0:T(8,128)(2,1)}, bf16[384,2048]{1,0:T(8,128)(2,1)}, u32[]{:S(2)}, u32[]{:S(2)}) %collective-permute-start.11) | collective-permute-done | bytes 1572896 | tf_op jit(solution)/shard_map/ppermute | solution.py:445
  335.6 5.0 %shard_map.144 = (bf16[2048,384]{1,0:T(8,128)(2,1)}, bf16[2048,384]{1,0:T(8,128)(2,1)}) custom-call(bf16[2048,768]{1,0:T(8,128)(2,1)} %get-tuple-element.69.a_ref, bf16[2048,768]{1,0:T(8,128)(2,1)} %collective-permute-done.10.b_ref, bf16[384,2048]{1,0:T(8,128)(2,1)} %shard_map.143.refs_0_), custom_call_target="tpu_custom_call" | custom-call | flops 1 | bytes 1 | tf_op jit(solution)/shard_map/pallas_call | solution.py:357
  340.6 15.8 %collective-permute-done.9 = bf16[256,2176]{1,0:T(8,128)(2,1)} collective-permute-done((bf16[256,2176]{1,0:T(8,128)(2,1)}, bf16[256,2176]{1,0:T(8,128)(2,1)}, u32[]{:S(2)}, u32[]{:S(2)}) %collective-permute-start.9) | collective-permute-done | bytes 1114144 | tf_op jit(solution)/shard_map/ppermute | solution.py:457
  (54 shorter events, 71.0 us)
Async XLA Ops:
  2.1 9.1 %copy-start.4 = (s32[1,256,2]{1,2,0:T(2,128)S(1)}, s32[1,256,2]{1,2,0:T(2,128)}, u32[]{:S(2)}) copy-start(s32[1,256,2]{1,2,0:T(2,128)} %param.12) | copy-start | bytes 6148
  5.4 53.2 %collective-permute-start = (bf16[528,2048]{1,0:T(8,128)(2,1)}, bf16[528,2048]{1,0:T(8,128)(2,1)}, u32[]{:S(2)}, u32[]{:S(2)}) collective-permute-start(bf16[528,2048]{1,0:T(8,128)(2,1)} %shard_map.128.refs_0_.refs_1_), channel_id=1, source_target_pairs={{0,4},{1,5},{2,6},{3,7},{4,8},{5,9},{6,10},{7,11},{8,12},{9,13},{1... | collective-permute-start | bytes 6488072 | tf_op jit(solution)/shard_map/ppermute | solution.py:388
  7.3 51.3 %collective-permute-start.2 = (bf16[528,2048]{1,0:T(8,128)(2,1)}, bf16[528,2048]{1,0:T(8,128)(2,1)}, u32[]{:S(2)}, u32[]{:S(2)}) collective-permute-start(bf16[528,2048]{1,0:T(8,128)(2,1)} %shard_map.128.refs_0_.refs_1_), channel_id=1, source_target_pairs={{0,28},{1,29},{2,30},{3,31},{4,0},{5,1},{6,2},{7,3},{8,4},{9,5},{1... | collective-permute-start | bytes 6488072 | tf_op jit(solution)/shard_map/ppermute | solution.py:389
  11.4 55.3 %copy-start.2 = (s32[256,2]{1,0:T(8,128)}, s32[256,2]{1,0:T(8,128)S(1)}, u32[]{:S(2)}) copy-start(s32[256,2]{1,0:T(8,128)S(1)} %bitcast_add_fusion.place_ref) | copy-start | bytes 6148
  11.4 5.1 %collective-permute-start.4 = (s32[256,2]{1,0:T(8,128)S(1)}, s32[256,2]{1,0:T(8,128)S(1)}, u32[]{:S(2)}, u32[]{:S(2)}) collective-permute-start(s32[256,2]{1,0:T(8,128)S(1)} %bitcast_add_fusion.place_ref), channel_id=1, source_target_pairs={{0,2},{1,3},{2,0},{3,1},{4,6},{5,7},{6,4},{7,5},{8,10},{9,11},{10,... | collective-permute-start | bytes 6152 | tf_op jit(solution)/shard_map/ppermute | solution.py:384
  16.5 0.6 copy-start.1
  21.2 45.5 %all-to-all-start = ((bf16[4,64,2048]{2,1,0:T(8,128)(2,1)}), bf16[4,64,2048]{2,1,0:T(8,128)(2,1)}, u32[]{:S(2)}, u32[]{:S(2)}) async-start(bf16[4,64,2048]{2,1,0:T(8,128)(2,1)} %bitcast.90), calls=%async_computation | async-start | bytes 2097152 | tf_op jit(solution)/shard_map/all_to_all | solution.py:394
  58.6 49.7 %collective-permute-start.1 = (bf16[528,2048]{1,0:T(8,128)(2,1)}, bf16[528,2048]{1,0:T(8,128)(2,1)}, u32[]{:S(2)}, u32[]{:S(2)}) collective-permute-start(bf16[528,2048]{1,0:T(8,128)(2,1)} %collective-permute-done.refs_0_.refs_2_), channel_id=1, source_target_pairs={{0,4},{1,5},{2,6},{3,7},{4,8},{5,9},{6,10},{7,11},{8,12},{9,13},{1... | collective-permute-start | bytes 6488072 | tf_op jit(solution)/shard_map/ppermute | solution.py:390
  58.6 49.7 %collective-permute-start.3 = (bf16[528,2048]{1,0:T(8,128)(2,1)}, bf16[528,2048]{1,0:T(8,128)(2,1)}, u32[]{:S(2)}, u32[]{:S(2)}) collective-permute-start(bf16[528,2048]{1,0:T(8,128)(2,1)} %collective-permute-done.2.refs_1_.refs_3_), channel_id=1, source_target_pairs={{0,28},{1,29},{2,30},{3,31},{4,0},{5,1},{6,2},{7,3},{8,4},{9,5},{1... | collective-permute-start | bytes 6488072 | tf_op jit(solution)/shard_map/ppermute | solution.py:391
  66.7 54.8 %all-to-all-start.1 = ((bf16[4,128,2048]{2,1,0:T(8,128)(2,1)}), bf16[4,128,2048]{2,1,0:T(8,128)(2,1)}, u32[]{:S(2)}, u32[]{:S(2)}) async-start(bf16[4,128,2048]{2,1,0:T(8,128)(2,1)} %bitcast.88), calls=%async_computation.1 | async-start | bytes 4194304 | tf_op jit(solution)/shard_map/all_to_all | solution.py:394
  113.4 36.2 %collective-permute-start.5 = (bf16[384,2048]{1,0:T(8,128)(2,1)}, bf16[384,2048]{1,0:T(8,128)(2,1)}, u32[]{:S(2)}, u32[]{:S(2)}) collective-permute-start(bf16[384,2048]{1,0:T(8,128)(2,1)} %get-tuple-element.40.refs_4_), channel_id=1, source_target_pairs={{0,4},{1,5},{2,6},{3,7},{4,8},{5,9},{6,10},{7,11},{8,12},{9,13},{1... | collective-permute-start | bytes 4718600 | tf_op jit(solution)/shard_map/ppermute | solution.py:425
  113.4 36.2 %collective-permute-start.6 = (bf16[384,2048]{1,0:T(8,128)(2,1)}, bf16[384,2048]{1,0:T(8,128)(2,1)}, u32[]{:S(2)}, u32[]{:S(2)}) collective-permute-start(bf16[384,2048]{1,0:T(8,128)(2,1)} %get-tuple-element.41), channel_id=1, source_target_pairs={{0,28},{1,29},{2,30},{3,31},{4,0},{5,1},{6,2},{7,3},{8,4},{9,5},{1... | collective-permute-start | bytes 4718600 | tf_op jit(solution)/shard_map/ppermute | solution.py:426
  121.5 32.4 %all-to-all-start.2 = ((bf16[4,128,2048]{2,1,0:T(8,128)(2,1)}), bf16[4,128,2048]{2,1,0:T(8,128)(2,1)}, u32[]{:S(2)}, u32[]{:S(2)}) async-start(bf16[4,128,2048]{2,1,0:T(8,128)(2,1)} %bitcast.87), calls=%async_computation.2 | async-start | bytes 4194304 | tf_op jit(solution)/shard_map/all_to_all | solution.py:394
  153.9 29.1 %all-to-all-start.4 = ((bf16[4,128,2048]{2,1,0:T(8,128)(2,1)}), bf16[4,128,2048]{2,1,0:T(8,128)(2,1)}, u32[]{:S(2)}, u32[]{:S(2)}) async-start(bf16[4,128,2048]{2,1,0:T(8,128)(2,1)} %bitcast.91), calls=%async_computation.4 | async-start | bytes 4194304 | tf_op jit(solution)/shard_map/all_to_all | solution.py:394
  158.8 15.4 %collective-permute-start.7 = (bf16[128,2048]{1,0:T(8,128)(2,1)}, bf16[128,2048]{1,0:T(8,128)(2,1)S(1)}, u32[]{:S(2)}, u32[]{:S(2)}) collective-permute-start(bf16[128,2048]{1,0:T(8,128)(2,1)} %get-tuple-element.47), channel_id=1, source_target_pairs={{0,4},{1,5},{2,6},{3,7},{4,8},{5,9},{6,10},{7,11},{8,12},{9,13},{1... | collective-permute-start | bytes 1572872 | tf_op jit(solution)/shard_map/ppermute | solution.py:433
  160.3 14.0 %collective-permute-start.8 = (bf16[128,2048]{1,0:T(8,128)(2,1)}, bf16[128,2048]{1,0:T(8,128)(2,1)}, u32[]{:S(2)}, u32[]{:S(2)}) collective-permute-start(bf16[128,2048]{1,0:T(8,128)(2,1)} %get-tuple-element.48), channel_id=1, source_target_pairs={{0,28},{1,29},{2,30},{3,31},{4,0},{5,1},{6,2},{7,3},{8,4},{9,5},{1... | collective-permute-start | bytes 1572872 | tf_op jit(solution)/shard_map/ppermute | solution.py:434
  174.2 0.8 copy-start
  183.0 18.8 %all-to-all-start.3 = ((bf16[4,64,2048]{2,1,0:T(8,128)(2,1)}), bf16[4,64,2048]{2,1,0:T(8,128)(2,1)}, u32[]{:S(2)}, u32[]{:S(2)}) async-start(bf16[4,64,2048]{2,1,0:T(8,128)(2,1)} %bitcast.89), calls=%async_computation.3 | async-start | bytes 2097152 | tf_op jit(solution)/shard_map/all_to_all | solution.py:394
  208.2 105.3 %all-to-all-start.5 = ((bf16[16,64,2176]{2,1,0:T(8,128)(2,1)}), bf16[16,64,2176]{2,1,0:T(8,128)(2,1)}, u32[]{:S(2)}, u32[]{:S(2)}) async-start(bf16[16,64,2176]{2,1,0:T(8,128)(2,1)} %bitcast.71), calls=%async_computation.5 | async-start | bytes 8912896 | tf_op jit(solution)/shard_map/all_to_all | solution.py:448
  223.1 112.5 %collective-permute-start.10 = (bf16[2048,768]{1,0:T(8,128)(2,1)}, bf16[2048,768]{1,0:T(8,128)(2,1)}, u32[]{:S(2)}, u32[]{:S(2)}) collective-permute-start(bf16[2048,768]{1,0:T(8,128)(2,1)} %get-tuple-element.69.a_ref), channel_id=1, source_target_pairs={{0,224},{32,192},{64,160},{96,128},{128,96},{160,64},{192,32},{224... | collective-permute-start | bytes 9437192 | tf_op jit(solution)/shard_map/ppermute | solution.py:446
  227.9 103.7 %collective-permute-start.11 = (bf16[384,2048]{1,0:T(8,128)(2,1)}, bf16[384,2048]{1,0:T(8,128)(2,1)}, u32[]{:S(2)}, u32[]{:S(2)}) collective-permute-start(bf16[384,2048]{1,0:T(8,128)(2,1)} %get-tuple-element.70.a_ref), channel_id=1, source_target_pairs={{0,224},{32,192},{64,160},{96,128},{128,96},{160,64},{192,32},{224... | collective-permute-start | bytes 4718600 | tf_op jit(solution)/shard_map/ppermute | solution.py:445
  318.5 38.0 %collective-permute-start.9 = (bf16[256,2176]{1,0:T(8,128)(2,1)}, bf16[256,2176]{1,0:T(8,128)(2,1)}, u32[]{:S(2)}, u32[]{:S(2)}) collective-permute-start(bf16[256,2176]{1,0:T(8,128)(2,1)} %shard_map.141.refs_0_), channel_id=1, source_target_pairs={{0,2},{1,3},{2,0},{3,1},{4,6},{5,7},{6,4},{7,5},{8,10},{9,11},{10,... | collective-permute-start | bytes 3342344 | tf_op jit(solution)/shard_map/ppermute | solution.py:457
  358.2 1.4 copy-start.3

commit v3 on v2

--- a/solution.py
+++ b/solution.py
@@ -132,39 +132,67 @@
 
 
 def pick_onward(sources, planes, most, after=()):
-    half = most // 2
-    low = 2 * LANES * most
-
     def body(routes, refs, outs):
         for d in range(2):
-            for t, rows in enumerate(pick(routes[d], planes[d][0], refs[d])):
+            for t, rows in enumerate(pick(routes[d], planes[d], refs[d])):
                 for r in range(LANES):
                     to = (2 * r + t) * most
                     outs[d][to : to + most, :] = rows[r * most : (r + 1) * most]
-            for t, rows in enumerate(pick(routes[d], planes[d][1], refs[d])):
+
+    return pick_call(body, sources, [2 * LANES * most] * 2, after)
+
+
+def pick_mid(sources, planes, beyond, most, after=()):
+    half = most // 2
+    size = 6 * most
+
+    def body(routes, refs, outs):
+        for d in range(2):
+            for t, rows in enumerate(pick(routes[d], planes[d], refs[d])):
                 for r in range(LANES):
-                    to, at = low + (2 * r + t) * half, r * most + d * half
-                    outs[d][to : to + half, :] = rows[at : at + half]
-
-    return pick_call(body, sources, [low + low // 2] * 2, after)
-
-
-def spread(up, down, rows, onward, after=()):
-    width = up.shape[1]
-    rest = up.shape[0] - rows
+                    to = r * size + (2 * d + t) * most
+                    outs[0][to : to + most, :] = rows[r * most : (r + 1) * most]
+            for t, rows in enumerate(pick(routes[d], beyond[d], refs[d])):
+                for r in range(LANES):
+                    to, at = r * size + 4 * most + (2 * d + t) * half, r * most + d * half
+                    outs[0][to : to + half, :] = rows[at : at + half]
+
+    return pick_call(body, sources, [LANES * size], after)[0]
+
+
+def beyond_rows(block, most):
+    rows, width = block.shape
     size = rows // LANES
 
+    def body(block_ref, *outs):
+        for r in range(LANES):
+            for d in range(2):
+                low = r * size + size - (2 - d) * most
+                outs[d][r * most : (r + 1) * most, :] = block_ref[low : low + most, :]
+
+    def columns(count):
+        return pl.BlockSpec((count, TILE), lambda i: (0, i))
+
+    return pl.pallas_call(
+        body,
+        grid=(width // TILE,),
+        out_shape=[jax.ShapeDtypeStruct((LANES * most, width), BF)] * 2,
+        in_specs=[columns(rows)],
+        out_specs=[columns(LANES * most)] * 2,
+        cost_estimate=LIGHT,
+        compiler_params=PARAMS,
+    )(block)
+
+
+def spread(up, down, after=()):
+    rows, width = up.shape
+    size = rows // LANES
+
     def body(up_ref, down_ref, *refs):
-        outs = refs[len(after) :]
         for r in range(LANES):
             for i, ref in enumerate((up_ref, down_ref)):
                 to = (2 * r + i) * size
-                outs[0][to : to + size, :] = ref[r * size : (r + 1) * size, :]
-        if onward:
-            outs[1][...] = up_ref[rows:, :]
-            outs[2][...] = down_ref[rows:, :]
-
-    shapes = [2 * rows] + [rest] * (2 * onward)
+                refs[-1][to : to + size, :] = ref[r * size : (r + 1) * size, :]
 
     def columns(count):
         return pl.BlockSpec((count, TILE), lambda i: (0, i))
@@ -172,9 +200,9 @@
     return pl.pallas_call(
         body,
         grid=(width // TILE,),
-        out_shape=[jax.ShapeDtypeStruct((n, width), BF) for n in shapes],
-        in_specs=[columns(up.shape[0])] * 2 + [ANYWHERE] * len(after),
-        out_specs=[columns(n) for n in shapes],
+        out_shape=jax.ShapeDtypeStruct((2 * rows, width), BF),
+        in_specs=[columns(rows)] * 2 + [ANYWHERE] * len(after),
+        out_specs=columns(2 * rows),
         cost_estimate=LIGHT,
         compiler_params=PARAMS,
     )(up, down, *after)
@@ -210,19 +238,16 @@
     )(jnp.stack(lane_info), place, back)
 
 
-def chunk_grads(block, run, start, total_rows, places, shared, weights, after=()):
-    rows, width = block.shape
-    rows = rows // LANES
-    size = rows // 2
-    count = LANES * size
+def chunk_grads(blocks, moves, count, start, total_rows, places, shared, weights, after=()):
+    width = blocks[0].shape[1]
     ff = weights[0].shape[1]
     most = 32
-    runs = size // run
-    n_in = 2 + 3 + len(after) + len(shared)
+    n_in = 1 + len(blocks) + 3 + len(after) + len(shared)
+    moves = sorted(moves, key=lambda move: move[2])
 
     def body(*refs):
         place_ref = refs[0]
-        gate_ref, up_ref, down_ref = refs[2:5]
+        gate_ref, up_ref, down_ref = refs[1 + len(blocks) : 4 + len(blocks)]
         outs = refs[n_in : n_in + 5]
         x, g, hid, d, dx, wg, wu, wd, sems, out_sems = refs[n_in + 5 :]
         loads = [
@@ -230,17 +255,14 @@
             pltpu.make_async_copy(up_ref, wu, sems.at[1]),
             pltpu.make_async_copy(down_ref, wd, sems.at[2]),
         ]
-        pieces = []
-        for t, into in enumerate((x, g)):
-            for r in range(LANES):
-                for i in range(runs):
-                    pieces.append(
-                        pltpu.make_async_copy(
-                            refs[1].at[pl.ds(r * rows + (2 * i + t) * run, run), :],
-                            into.at[pl.ds(r * size + i * run, run), :],
-                            sems.at[3 + len(pieces)],
-                        )
-                    )
+        pieces = [
+            pltpu.make_async_copy(
+                refs[1 + b].at[pl.ds(at, size), :],
+                (x, g)[t].at[pl.ds(to, size), :],
+                sems.at[3 + i],
+            )
+            for i, (b, at, t, to, size) in enumerate(moves)
+        ]
         split = len(pieces) // 2
         for copy in pieces[:split] + loads[:2] + pieces[split:] + loads[2:]:
             copy.start()
@@ -287,7 +309,7 @@
             copy.wait()
 
     shapes = [width, width, ff, 2 * ff, width + SCORE]
-    first = 5 + len(after)
+    first = 4 + len(blocks) + len(after)
     return pl.pallas_call(
         body,
         out_shape=[jax.ShapeDtypeStruct((total_rows, n), BF) for n in shapes],
@@ -303,12 +325,12 @@
             pltpu.VMEM((width, ff), BF),
             pltpu.VMEM((width, ff), BF),
             pltpu.VMEM((ff, width), BF),
-            pltpu.SemaphoreType.DMA((3 + 2 * LANES * runs,)),
+            pltpu.SemaphoreType.DMA((3 + len(moves),)),
             pltpu.SemaphoreType.DMA((4 + count // most,)),
         ],
         cost_estimate=LIGHT,
         compiler_params=PARAMS,
-    )(places, block, *weights, *after, *shared)
+    )(places, *blocks, *weights, *after, *shared)
 
 
 def weight_grads(x, d, hidden, g):
@@ -396,8 +418,8 @@
         )
 
     slot_count = experts * most
-    offsets_of = ((0,), (-1, 1), (-2, 2), (-3, 3), (4,))
-    starts = [b * LANES * most for b in (0, 1, 3, 5, 7)]
+    offsets_of = ((0,), (-1, 1), (-2, 2), (-3, 3, 4))
+    starts = [b * LANES * most for b in (0, 1, 3, 5)]
 
     def places(offsets):
         found = []
@@ -409,35 +431,58 @@
 
     expert_weights = (weight_gate, weight_up, weight_down)
 
-    def work(i, blocks, run, shared, after=()):
+    half = most // 2
+
+    def moves_of(stride, sources, per_lane):
+        return [
+            (0, r * stride + (2 * i + t) * most, t, (r * per_lane + i) * most, most)
+            for r in range(LANES)
+            for i in range(sources)
+            for t in range(2)
+        ]
+
+    def work(i, blocks, moves, shared, after=()):
+        count = LANES * most * len(offsets_of[i])
         return chunk_grads(
-            blocks, run, starts[i], slot_count, places(offsets_of[i]), shared, expert_weights, after
+            blocks,
+            moves,
+            count,
+            starts[i],
+            slot_count,
+            places(offsets_of[i]),
+            shared,
+            expert_weights,
+            after,
         )
 
     own_out = pick_lanes([own], [0], most, after=[place_across])
     here_rows = exchange(own_out)
-    shared = work(0, here_rows, most, [])
+    shared = work(0, [here_rows], moves_of(2 * most, 1, 1), [])
     near_out = pick_lanes([plus1, minus1], [1, RING - 1], most, after=[own_out])
     near = exchange(near_out)
+    mid_out = pick_mid(
+        [plus2, minus2], [2, RING - 2], [4, RING - 4], most, after=[near_out, shared[4]]
+    )
     onward_up, onward_down = pick_onward(
-        [plus2, minus2], [[3, 4], [RING - 3, RING - 4]], most, after=[near_out, shared[4]]
+        [plus2, minus2], [3, RING - 3], most, after=[mid_out]
     )
     plus3 = lax.ppermute(onward_up, "expert", up_ring)
     minus3 = lax.ppermute(onward_down, "expert", down_ring)
-    mid_out = pick_lanes([plus2, minus2], [2, RING - 2], most, after=[onward_up])
     mid = exchange(mid_out)
-    shared = work(1, near, most, shared, after=[mid_out])
-    far_out, last_up, last_down = spread(
-        plus3, minus3, 2 * LANES * most, True, after=[shared[4]]
-    )
-    plus4 = lax.ppermute(last_up, "expert", up_ring)
-    minus4 = lax.ppermute(last_down, "expert", down_ring)
+    shared = work(1, [near], moves_of(4 * most, 2, 2), shared, after=[onward_up])
+    last_up, last_down = beyond_rows(mid, most)
+    plus4 = lax.ppermute(last_up, "expert", ring_step(2))
+    minus4 = lax.ppermute(last_down, "expert", ring_step(-2))
+    far_out = spread(plus3, minus3, after=[shared[4]])
     far = exchange(far_out)
-    shared = work(2, mid, most, shared, after=[far_out])
-    (last_out,) = spread(plus4, minus4, LANES * most, False, after=[shared[4]])
-    last = exchange(last_out)
-    shared = work(3, far, most, shared, after=[last_out])
-    shared = work(4, last, most // 2, shared)
+    shared = work(2, [mid], moves_of(6 * most, 2, 2), shared, after=[far_out, last_up])
+    last_moves = [
+        (1 + d, r * most + t * half, t, (3 * r + 2) * most + d * half, half)
+        for r in range(LANES)
+        for d in range(2)
+        for t in range(2)
+    ]
+    shared = work(3, [far, plus4, minus4], moves_of(4 * most, 2, 3) + last_moves, shared)
 
     x_all, g_all, hidden, d_rows, dx = shared
     down_part, in_parts = weight_grads(x_all, d_rows, hidden, g_all)

time: 362 us -> 355 us (0.981)
  starting transfers between devices: 54.4 us -> 47 us
  waiting for transfers between devices: 201 us -> 206 us
  Pallas kernels: 93 us -> 88.4 us
    ppermute x1, waiting for transfers between devices: 32.7 us -> 0.01 us  [per_device(): plus1 = lax.ppermute(own, 'expert', up_ring)]
    ppermute x1, waiting for transfers between devices: 0.01 us -> 31.9 us  [per_device(): minus1 = lax.ppermute(own, 'expert', down_ring)]
    ppermute x1, waiting for transfers between devices: 0.01 us -> 28.9 us  [per_device(): minus2 = lax.ppermute(minus1, 'expert', down_ring)]
    ppermute x1, waiting for transfers between devices: 29.7 us -> 3.42 us  [per_device(): plus2 = lax.ppermute(plus1, 'expert', up_ring)]
    ppermute x1, waiting for transfers between devices: 0.01 us -> 15.5 us  [per_device(): minus3 = lax.ppermute(onward_down, 'expert', down_ring)]
    ppermute x1, waiting for transfers between devices: 15 us -> 1.47 us  [per_device(): plus3 = lax.ppermute(onward_up, 'expert', up_ring)]
    pallas_call x5 -> x4, Pallas kernels: 34.9 us -> 30.3 us  [chunk_grads(): pl.pallas_call(body, out_shape=[jax.ShapeDtypeStruct((total_rows, n), BF)...]
    all_to_all x5 -> x4, starting transfers between devices: 25.5 us -> 20.9 us  [exchange(): lax.all_to_all(block, 'expert', 0, 0, tiled=True, axis_index_groups=PLANE...]
  transfers between devices with their start and end apart: 18 -> 17, of which waited for: 11 -> 12; matrix products, arithmetic and copies ran while one was open for 1% -> 1% of each run, Pallas kernels for 23% -> 22%
where the time goes in v3:
time: 355 us; the launch traced here: 352 us
  waiting for transfers between devices  206 us (58%)
  Pallas kernels  88.4 us (25%)
  starting transfers between devices  47 us (13%)
  local copies, waits for them, and re-layouts  5.32 us (1%)
  other arithmetic  4.47 us (1%)
    all_to_all x1, waiting for transfers between devices, per_device(): lax.all_to_all(dx.reshape(2 * RING, 2 * most, width + SCORE), 'expert', 0...  84.2 us
    ppermute x1, waiting for transfers between devices, per_device(): minus1 = lax.ppermute(own, 'expert', down_ring)  31.9 us
    pallas_call x4, Pallas kernels, chunk_grads(): pl.pallas_call(body, out_shape=[jax.ShapeDtypeStruct((total_rows, n), BF)...  30.3 us
    ppermute x1, waiting for transfers between devices, per_device(): minus2 = lax.ppermute(minus1, 'expert', down_ring)  28.9 us
    all_to_all x4, starting transfers between devices, exchange(): lax.all_to_all(block, 'expert', 0, 0, tiled=True, axis_index_groups=PLANE...  20.9 us
    pallas_call x4, Pallas kernels, pick_call(): pl.pallas_call(inner, grid=(width // TILE,), out_shape=[jax.ShapeDtypeStr...  18.9 us
    ppermute x1, waiting for transfers between devices, per_device(): minus3 = lax.ppermute(onward_down, 'expert', down_ring)  15.5 us
    ppermute x1, waiting for transfers between devices, per_device(): away = lax.ppermute(leaving, 'expert', ACROSS)  14.5 us
  transfers between devices with their start and end apart: 17, of which 12 were waited for; matrix products, arithmetic and copies ran while one was open for 1% of the time, Pallas kernels for 22%

profile of v3, /device:TPU:2, one launch (start us, length us, event | category | flops | bytes accessed | tf_op | source)
XLA Modules:
  0.0 352.2 jit_solution(1141038461693657696)
XLA Ops:
  5.4 5.9 %collective-permute-start.2 = (bf16[528,2048]{1,0:T(8,128)(2,1)}, bf16[528,2048]{1,0:T(8,128)(2,1)}, u32[]{:S(2)}, u32[]{:S(2)}) collective-permute-start(bf16[528,2048]{1,0:T(8,128)(2,1)} %shard_map.128.refs_0_.refs_1_), channel_id=1, source_target_pairs={{0,28},{1,29},{2,30},{3,31},{4,0},{5,1},{6,2},{7,3},{8,4},{9,5},{1... | collective-permute-start | bytes 6488072 | tf_op jit(solution)/shard_map/ppermute | solution.py:411
  26.0 31.9 %collective-permute-done.2.refs_1_.refs_3_ = bf16[528,2048]{1,0:T(8,128)(2,1)} collective-permute-done((bf16[528,2048]{1,0:T(8,128)(2,1)}, bf16[528,2048]{1,0:T(8,128)(2,1)}, u32[]{:S(2)}, u32[]{:S(2)}) %collective-permute-start.2) | collective-permute-done | bytes 2162720 | tf_op jit(solution)/shard_map/ppermute | solution.py:411
  61.6 4.8 %shard_map.130.refs_4_ = bf16[512,2048]{1,0:T(8,128)(2,1)} custom-call(bf16[528,2048]{1,0:T(8,128)(2,1)} %collective-permute-done.refs_0_.refs_2_, bf16[528,2048]{1,0:T(8,128)(2,1)} %collective-permute-done.2.refs_1_.refs_3_, bf16[528,2048]{1,0:T(8,128)(2,1)} %collective-permute-done.refs_0_.refs_2_, ...), custom_call_target="tpu_custom_call" | custom-call | flops 1 | bytes 1 | tf_op jit(solution)/shard_map/pallas_call | solution.py:108
  66.4 5.0 %all-to-all-start.1 = ((bf16[4,128,2048]{2,1,0:T(8,128)(2,1)}), bf16[4,128,2048]{2,1,0:T(8,128)(2,1)}, u32[]{:S(2)}, u32[]{:S(2)}) async-start(bf16[4,128,2048]{2,1,0:T(8,128)(2,1)} %bitcast.83), calls=%async_computation.1 | async-start | bytes 4194304 | tf_op jit(solution)/shard_map/all_to_all | solution.py:416
  72.0 6.4 %shard_map.131 = (bf16[1024,2048]{1,0:T(8,128)(2,1)}, bf16[1024,2048]{1,0:T(8,128)(2,1)}, bf16[1024,384]{1,0:T(8,128)(2,1)}, bf16[1024,768]{1,0:T(8,128)(2,1)}, bf16[1024,2176]{1,0:T(8,128)(2,1)}) custom-call(s32[4]{0:T(128)} %pad_add_fusion.1.refs_0_, bf16[256,2048]{1,0:T(8,128)(2,1)} %bitcast.27.refs_1_, bf16[2048,384]{1,0:T(8,128)(2,1)} %bitcast.71, ...), custom_call_target="tpu_custom_call" | custom-call | flops 1 | bytes 1 | tf_op jit(solution)/shard_map/pallas_call | solution.py:313
  78.4 28.9 %collective-permute-done.3.refs_1_.refs_3_ = bf16[528,2048]{1,0:T(8,128)(2,1)} collective-permute-done((bf16[528,2048]{1,0:T(8,128)(2,1)}, bf16[528,2048]{1,0:T(8,128)(2,1)}, u32[]{:S(2)}, u32[]{:S(2)}) %collective-permute-start.3) | collective-permute-done | bytes 2162720 | tf_op jit(solution)/shard_map/ppermute | solution.py:413
  110.7 5.4 %shard_map.132.refs_4_ = bf16[768,2048]{1,0:T(8,128)(2,1)} custom-call(bf16[528,2048]{1,0:T(8,128)(2,1)} %collective-permute-done.1.refs_0_.refs_2_, bf16[528,2048]{1,0:T(8,128)(2,1)} %collective-permute-done.3.refs_1_.refs_3_, bf16[528,2048]{1,0:T(8,128)(2,1)} %collective-permute-done.1.refs_0_.refs_2_, ...), custom_call_target="tpu_custom_call" | custom-call | flops 1 | bytes 1 | tf_op jit(solution)/shard_map/pallas_call | solution.py:108
  116.1 5.2 %all-to-all-start.3 = ((bf16[4,192,2048]{2,1,0:T(8,128)(2,1)}), bf16[4,192,2048]{2,1,0:T(8,128)(2,1)}, u32[]{:S(2)}, u32[]{:S(2)}) async-start(bf16[4,192,2048]{2,1,0:T(8,128)(2,1)} %bitcast.70), calls=%async_computation.3 | async-start | bytes 6291456 | tf_op jit(solution)/shard_map/all_to_all | solution.py:416
  128.6 7.4 %shard_map.134 = (bf16[1024,2048]{1,0:T(8,128)(2,1)}, bf16[1024,2048]{1,0:T(8,128)(2,1)}, bf16[1024,384]{1,0:T(8,128)(2,1)}, bf16[1024,768]{1,0:T(8,128)(2,1)}, bf16[1024,2176]{1,0:T(8,128)(2,1)}) custom-call(s32[8]{0:T(128)} %stack.159.refs_0_, ...), custom_call_target="tpu_custom_call", output_to_operand_aliasing={{0}: (6, {}), {1}: (7, {}), {2}: (8, {}), {3}: (9, {}), {4}... | custom-call | flops 1 | bytes 1 | tf_op jit(solution)/shard_map/pallas_call | solution.py:313
  136.0 15.5 %collective-permute-done.6.down_ref = bf16[256,2048]{1,0:T(8,128)(2,1)} collective-permute-done((bf16[256,2048]{1,0:T(8,128)(2,1)}, bf16[256,2048]{1,0:T(8,128)(2,1)}, u32[]{:S(2)}, u32[]{:S(2)}) %collective-permute-start.6) | collective-permute-done | bytes 1048608 | tf_op jit(solution)/shard_map/ppermute | solution.py:470
  156.8 6.0 %all-to-all-start.2 = ((bf16[4,128,2048]{2,1,0:T(8,128)(2,1)}), bf16[4,128,2048]{2,1,0:T(8,128)(2,1)}, u32[]{:S(2)}, u32[]{:S(2)}) async-start(bf16[4,128,2048]{2,1,0:T(8,128)(2,1)} %bitcast.84), calls=%async_computation.2 | async-start | bytes 4194304 | tf_op jit(solution)/shard_map/all_to_all | solution.py:416
  170.7 7.4 %shard_map.137 = (bf16[1024,2048]{1,0:T(8,128)(2,1)}, bf16[1024,2048]{1,0:T(8,128)(2,1)}, bf16[1024,384]{1,0:T(8,128)(2,1)}, bf16[1024,768]{1,0:T(8,128)(2,1)}, bf16[1024,2176]{1,0:T(8,128)(2,1)}) custom-call(s32[8]{0:T(128)} %stack.168.refs_0_, ...), custom_call_target="tpu_custom_call", output_to_operand_aliasing={{0}: (7, {}), {1}: (8, {}), {2}: (9, {}), {3}: (10, {}), {4... | custom-call | flops 1 | bytes 1 | tf_op jit(solution)/shard_map/pallas_call | solution.py:313
  178.1 8.8 %all-to-all-done.2 = bf16[4,128,2048]{2,1,0:T(8,128)(2,1)} async-done(((bf16[4,128,2048]{2,1,0:T(8,128)(2,1)}), bf16[4,128,2048]{2,1,0:T(8,128)(2,1)}, u32[]{:S(2)}, u32[]{:S(2)}) %all-to-all-start.2) | async-done | bytes 2097184 | tf_op jit(solution)/shard_map/all_to_all | solution.py:416
  186.9 4.9 %collective-permute-done.8.refs_3_ = bf16[128,2048]{1,0:T(8,128)(2,1)S(1)} collective-permute-done((bf16[128,2048]{1,0:T(8,128)(2,1)}, bf16[128,2048]{1,0:T(8,128)(2,1)S(1)}, u32[]{:S(2)}, u32[]{:S(2)}) %collective-permute-start.8) | collective-permute-done | bytes 524320 | tf_op jit(solution)/shard_map/ppermute | solution.py:475
  192.8 9.1 %shard_map.138 = (bf16[1024,2048]{1,0:T(8,128)(2,1)}, bf16[1024,2048]{1,0:T(8,128)(2,1)}, bf16[1024,384]{1,0:T(8,128)(2,1)}, bf16[1024,768]{1,0:T(8,128)(2,1)}, bf16[1024,2176]{1,0:T(8,128)(2,1)}) custom-call(s32[12]{0:T(128)} %stack.145.refs_0_, ...), custom_call_target="tpu_custom_call", output_to_operand_aliasing={{0}: (7, {}), {1}: (8, {}), {2}: (9, {}), {3}: (10, {}), {4... | custom-call | flops 1 | bytes 1 | tf_op jit(solution)/shard_map/pallas_call | solution.py:313
  201.9 5.0 %all-to-all-start.4 = ((bf16[16,64,2176]{2,1,0:T(8,128)(2,1)}), bf16[16,64,2176]{2,1,0:T(8,128)(2,1)}, u32[]{:S(2)}, u32[]{:S(2)}) async-start(bf16[16,64,2176]{2,1,0:T(8,128)(2,1)} %bitcast.69), calls=%async_computation.4 | async-start | bytes 8912896 | tf_op jit(solution)/shard_map/all_to_all | solution.py:493
  206.9 9.5 %shard_map.141 = (bf16[384,2048]{1,0:T(8,128)(2,1)}, bf16[2048,768]{1,0:T(8,128)(2,1)}) custom-call(bf16[1024,2048]{1,0:T(8,128)(2,1)} %get-tuple-element.53.x_ref, bf16[1024,768]{1,0:T(8,128)(2,1)} %get-tuple-element.54.d_ref, bf16[1024,384]{1,0:T(8,128)(2,1)} %get-tuple-element.55.hidden_ref, bf16[1024,2048]{1,0:T(8,128)(2,1)} %get-tuple-element.56.g_ref), custom_call_target="tpu_custom_call" | custom-call | flops 1 | bytes 1 | tf_op jit(solution)/shard_map/pallas_call | solution.py:350
  216.4 4.8 %collective-permute-start.10 = (bf16[2048,768]{1,0:T(8,128)(2,1)}, bf16[2048,768]{1,0:T(8,128)(2,1)}, u32[]{:S(2)}, u32[]{:S(2)}) collective-permute-start(bf16[2048,768]{1,0:T(8,128)(2,1)} %get-tuple-element.57.a_ref), channel_id=1, source_target_pairs={{0,224},{32,192},{64,160},{96,128},{128,96},{160,64},{192,32},{224... | collective-permute-start | bytes 9437192 | tf_op jit(solution)/shard_map/ppermute | solution.py:491
  222.6 84.2 %all-to-all-done.4 = bf16[16,64,2176]{2,1,0:T(8,128)(2,1)} async-done(((bf16[16,64,2176]{2,1,0:T(8,128)(2,1)}), bf16[16,64,2176]{2,1,0:T(8,128)(2,1)}, u32[]{:S(2)}, u32[]{:S(2)}) %all-to-all-start.4) | async-done | bytes 4456480 | tf_op jit(solution)/shard_map/all_to_all | solution.py:493
  306.8 4.9 %shard_map.140.refs_0_ = bf16[256,2176]{1,0:T(8,128)(2,1)} custom-call(s32[2]{0:T(128)} %pad_add_fusion.2.info_ref, s32[256,2]{1,0:T(8,128)} %copy-done.1, bf16[1024,2176]{1,0:T(8,128)(2,1)} %bitcast.54.back_ref), custom_call_target="tpu_custom_call" | custom-call | flops 1 | bytes 1 | tf_op jit(solution)/shard_map/pallas_call | solution.py:231
  312.6 5.0 %shard_map.139 = bf16[256,2176]{1,0:T(8,128)(2,1)} custom-call(s32[2]{0:T(128)} %pad_add_fusion.info_ref, s32[256,2]{1,0:T(8,128)} %copy-done.2, bf16[1024,2176]{1,0:T(8,128)(2,1)} %bitcast.54.back_ref), custom_call_target="tpu_custom_call" | custom-call | flops 1 | bytes 1 | tf_op jit(solution)/shard_map/pallas_call | solution.py:231
  317.6 7.3 %collective-permute-done.11.b_ref = bf16[384,2048]{1,0:T(8,128)(2,1)} collective-permute-done((bf16[384,2048]{1,0:T(8,128)(2,1)}, bf16[384,2048]{1,0:T(8,128)(2,1)}, u32[]{:S(2)}, u32[]{:S(2)}) %collective-permute-start.11) | collective-permute-done | bytes 1572896 | tf_op jit(solution)/shard_map/ppermute | solution.py:490
  328.9 5.0 %shard_map.143 = (bf16[2048,384]{1,0:T(8,128)(2,1)}, bf16[2048,384]{1,0:T(8,128)(2,1)}) custom-call(bf16[2048,768]{1,0:T(8,128)(2,1)} %get-tuple-element.57.a_ref, bf16[2048,768]{1,0:T(8,128)(2,1)} %collective-permute-done.10.b_ref, bf16[384,2048]{1,0:T(8,128)(2,1)} %shard_map.142.refs_0_), custom_call_target="tpu_custom_call" | custom-call | flops 1 | bytes 1 | tf_op jit(solution)/shard_map/pallas_call | solution.py:379
  333.9 14.5 %collective-permute-done.9 = bf16[256,2176]{1,0:T(8,128)(2,1)} collective-permute-done((bf16[256,2176]{1,0:T(8,128)(2,1)}, bf16[256,2176]{1,0:T(8,128)(2,1)}, u32[]{:S(2)}, u32[]{:S(2)}) %collective-permute-start.9) | collective-permute-done | bytes 1114144 | tf_op jit(solution)/shard_map/ppermute | solution.py:502
  (50 shorter events, 58.8 us)
Async XLA Ops:
  2.1 9.2 %copy-start.4 = (s32[1,256,2]{1,2,0:T(2,128)S(1)}, s32[1,256,2]{1,2,0:T(2,128)}, u32[]{:S(2)}) copy-start(s32[1,256,2]{1,2,0:T(2,128)} %param.12) | copy-start | bytes 6148
  5.4 52.5 %collective-permute-start.2 = (bf16[528,2048]{1,0:T(8,128)(2,1)}, bf16[528,2048]{1,0:T(8,128)(2,1)}, u32[]{:S(2)}, u32[]{:S(2)}) collective-permute-start(bf16[528,2048]{1,0:T(8,128)(2,1)} %shard_map.128.refs_0_.refs_1_), channel_id=1, source_target_pairs={{0,28},{1,29},{2,30},{3,31},{4,0},{5,1},{6,2},{7,3},{8,4},{9,5},{1... | collective-permute-start | bytes 6488072 | tf_op jit(solution)/shard_map/ppermute | solution.py:411
  11.3 50.3 %collective-permute-start = (bf16[528,2048]{1,0:T(8,128)(2,1)}, bf16[528,2048]{1,0:T(8,128)(2,1)}, u32[]{:S(2)}, u32[]{:S(2)}) collective-permute-start(bf16[528,2048]{1,0:T(8,128)(2,1)} %shard_map.128.refs_0_.refs_1_), channel_id=1, source_target_pairs={{0,4},{1,5},{2,6},{3,7},{4,8},{5,9},{6,10},{7,11},{8,12},{9,13},{1... | collective-permute-start | bytes 6488072 | tf_op jit(solution)/shard_map/ppermute | solution.py:410
  11.4 55.0 %copy-start.2 = (s32[256,2]{1,0:T(8,128)}, s32[256,2]{1,0:T(8,128)S(1)}, u32[]{:S(2)}) copy-start(s32[256,2]{1,0:T(8,128)S(1)} %bitcast_add_fusion.place_ref) | copy-start | bytes 6148
  11.5 5.1 %collective-permute-start.4 = (s32[256,2]{1,0:T(8,128)S(1)}, s32[256,2]{1,0:T(8,128)S(1)}, u32[]{:S(2)}, u32[]{:S(2)}) collective-permute-start(s32[256,2]{1,0:T(8,128)S(1)} %bitcast_add_fusion.place_ref), channel_id=1, source_target_pairs={{0,2},{1,3},{2,0},{3,1},{4,6},{5,7},{6,4},{7,5},{8,10},{9,11},{10,... | collective-permute-start | bytes 6152 | tf_op jit(solution)/shard_map/ppermute | solution.py:406
  16.5 0.7 copy-start.1
  21.2 45.2 %all-to-all-start = ((bf16[4,64,2048]{2,1,0:T(8,128)(2,1)}), bf16[4,64,2048]{2,1,0:T(8,128)(2,1)}, u32[]{:S(2)}, u32[]{:S(2)}) async-start(bf16[4,64,2048]{2,1,0:T(8,128)(2,1)} %bitcast.85), calls=%async_computation | async-start | bytes 2097152 | tf_op jit(solution)/shard_map/all_to_all | solution.py:416
  57.9 49.4 %collective-permute-start.3 = (bf16[528,2048]{1,0:T(8,128)(2,1)}, bf16[528,2048]{1,0:T(8,128)(2,1)}, u32[]{:S(2)}, u32[]{:S(2)}) collective-permute-start(bf16[528,2048]{1,0:T(8,128)(2,1)} %collective-permute-done.2.refs_1_.refs_3_), channel_id=1, source_target_pairs={{0,28},{1,29},{2,30},{3,31},{4,0},{5,1},{6,2},{7,3},{8,4},{9,5},{1... | collective-permute-start | bytes 6488072 | tf_op jit(solution)/shard_map/ppermute | solution.py:413
  61.6 49.1 %collective-permute-start.1 = (bf16[528,2048]{1,0:T(8,128)(2,1)}, bf16[528,2048]{1,0:T(8,128)(2,1)}, u32[]{:S(2)}, u32[]{:S(2)}) collective-permute-start(bf16[528,2048]{1,0:T(8,128)(2,1)} %collective-permute-done.refs_0_.refs_2_), channel_id=1, source_target_pairs={{0,4},{1,5},{2,6},{3,7},{4,8},{5,9},{6,10},{7,11},{8,12},{9,13},{1... | collective-permute-start | bytes 6488072 | tf_op jit(solution)/shard_map/ppermute | solution.py:412
  66.4 49.7 %all-to-all-start.1 = ((bf16[4,128,2048]{2,1,0:T(8,128)(2,1)}), bf16[4,128,2048]{2,1,0:T(8,128)(2,1)}, u32[]{:S(2)}, u32[]{:S(2)}) async-start(bf16[4,128,2048]{2,1,0:T(8,128)(2,1)} %bitcast.83), calls=%async_computation.1 | async-start | bytes 4194304 | tf_op jit(solution)/shard_map/all_to_all | solution.py:416
  116.1 40.7 %all-to-all-start.3 = ((bf16[4,192,2048]{2,1,0:T(8,128)(2,1)}), bf16[4,192,2048]{2,1,0:T(8,128)(2,1)}, u32[]{:S(2)}, u32[]{:S(2)}) async-start(bf16[4,192,2048]{2,1,0:T(8,128)(2,1)} %bitcast.70), calls=%async_computation.3 | async-start | bytes 6291456 | tf_op jit(solution)/shard_map/all_to_all | solution.py:416
  125.9 25.5 %collective-permute-start.6 = (bf16[256,2048]{1,0:T(8,128)(2,1)}, bf16[256,2048]{1,0:T(8,128)(2,1)}, u32[]{:S(2)}, u32[]{:S(2)}) collective-permute-start(bf16[256,2048]{1,0:T(8,128)(2,1)} %get-tuple-element.35), channel_id=1, source_target_pairs={{0,28},{1,29},{2,30},{3,31},{4,0},{5,1},{6,2},{7,3},{8,4},{9,5},{1... | collective-permute-start | bytes 3145736 | tf_op jit(solution)/shard_map/ppermute | solution.py:470
  126.2 26.7 %collective-permute-start.5 = (bf16[256,2048]{1,0:T(8,128)(2,1)}, bf16[256,2048]{1,0:T(8,128)(2,1)}, u32[]{:S(2)}, u32[]{:S(2)}) collective-permute-start(bf16[256,2048]{1,0:T(8,128)(2,1)} %get-tuple-element.34.refs_5_), channel_id=1, source_target_pairs={{0,4},{1,5},{2,6},{3,7},{4,8},{5,9},{6,10},{7,11},{8,12},{9,13},{1... | collective-permute-start | bytes 3145736 | tf_op jit(solution)/shard_map/ppermute | solution.py:469
  156.8 30.1 %all-to-all-start.2 = ((bf16[4,128,2048]{2,1,0:T(8,128)(2,1)}), bf16[4,128,2048]{2,1,0:T(8,128)(2,1)}, u32[]{:S(2)}, u32[]{:S(2)}) async-start(bf16[4,128,2048]{2,1,0:T(8,128)(2,1)} %bitcast.84), calls=%async_computation.2 | async-start | bytes 4194304 | tf_op jit(solution)/shard_map/all_to_all | solution.py:416
  166.5 25.3 %collective-permute-start.8 = (bf16[128,2048]{1,0:T(8,128)(2,1)}, bf16[128,2048]{1,0:T(8,128)(2,1)S(1)}, u32[]{:S(2)}, u32[]{:S(2)}) collective-permute-start(bf16[128,2048]{1,0:T(8,128)(2,1)} %get-tuple-element.42), channel_id=1, source_target_pairs={{0,24},{1,25},{2,26},{3,27},{4,28},{5,29},{6,30},{7,31},{8,0},{9,1... | collective-permute-start | bytes 1572872 | tf_op jit(solution)/shard_map/ppermute | solution.py:475
  166.5 26.2 %collective-permute-start.7 = (bf16[128,2048]{1,0:T(8,128)(2,1)}, bf16[128,2048]{1,0:T(8,128)(2,1)}, u32[]{:S(2)}, u32[]{:S(2)}) collective-permute-start(bf16[128,2048]{1,0:T(8,128)(2,1)} %get-tuple-element.41.refs_6_), channel_id=1, source_target_pairs={{0,8},{1,9},{2,10},{3,11},{4,12},{5,13},{6,14},{7,15},{8,16},{9,17... | collective-permute-start | bytes 1572872 | tf_op jit(solution)/shard_map/ppermute | solution.py:474
  191.8 0.9 copy-start
  201.9 104.9 %all-to-all-start.4 = ((bf16[16,64,2176]{2,1,0:T(8,128)(2,1)}), bf16[16,64,2176]{2,1,0:T(8,128)(2,1)}, u32[]{:S(2)}, u32[]{:S(2)}) async-start(bf16[16,64,2176]{2,1,0:T(8,128)(2,1)} %bitcast.69), calls=%async_computation.4 | async-start | bytes 8912896 | tf_op jit(solution)/shard_map/all_to_all | solution.py:493
  216.4 112.5 %collective-permute-start.10 = (bf16[2048,768]{1,0:T(8,128)(2,1)}, bf16[2048,768]{1,0:T(8,128)(2,1)}, u32[]{:S(2)}, u32[]{:S(2)}) collective-permute-start(bf16[2048,768]{1,0:T(8,128)(2,1)} %get-tuple-element.57.a_ref), channel_id=1, source_target_pairs={{0,224},{32,192},{64,160},{96,128},{128,96},{160,64},{192,32},{224... | collective-permute-start | bytes 9437192 | tf_op jit(solution)/shard_map/ppermute | solution.py:491
  221.2 103.7 %collective-permute-start.11 = (bf16[384,2048]{1,0:T(8,128)(2,1)}, bf16[384,2048]{1,0:T(8,128)(2,1)}, u32[]{:S(2)}, u32[]{:S(2)}) collective-permute-start(bf16[384,2048]{1,0:T(8,128)(2,1)} %get-tuple-element.58.a_ref), channel_id=1, source_target_pairs={{0,224},{32,192},{64,160},{96,128},{128,96},{160,64},{192,32},{224... | collective-permute-start | bytes 4718600 | tf_op jit(solution)/shard_map/ppermute | solution.py:490
  311.7 36.7 %collective-permute-start.9 = (bf16[256,2176]{1,0:T(8,128)(2,1)}, bf16[256,2176]{1,0:T(8,128)(2,1)}, u32[]{:S(2)}, u32[]{:S(2)}) collective-permute-start(bf16[256,2176]{1,0:T(8,128)(2,1)} %shard_map.140.refs_0_), channel_id=1, source_target_pairs={{0,2},{1,3},{2,0},{3,1},{4,6},{5,7},{6,4},{7,5},{8,10},{9,11},{10,... | collective-permute-start | bytes 3342344 | tf_op jit(solution)/shard_map/ppermute | solution.py:502
  350.2 1.4 copy-start.3

commit v4 on v3

--- a/solution.py
+++ b/solution.py
@@ -38,7 +38,7 @@
 WHOLE = pl.BlockSpec(memory_space=pltpu.VMEM)
 LIGHT = pl.CostEstimate(flops=1, bytes_accessed=1, transcendentals=0)
 PARAMS = pltpu.CompilerParams(vmem_limit_bytes=63 * 1024 * 1024)
-TILE = 512
+TILE = 1024
 
 
 def route_rows(acts, grads, source_row, experts_of, combine, me):

time: 355 us -> 352 us (level)
  Pallas kernels: 88.4 us -> 81.6 us
  waiting for transfers between devices: 206 us -> 211 us
    pallas_call x4, Pallas kernels: 18.9 us -> 14.3 us  [pick_call(): pl.pallas_call(inner, grid=(width // TILE,), out_shape=[jax.ShapeDtypeStr...]
  transfers between devices with their start and end apart: 17 -> 17, of which waited for: 12 -> 13; matrix products, arithmetic and copies ran while one was open for 1% -> 1% of each run, Pallas kernels for 22% -> 20%
where the time goes in v4:
time: 352 us; the launch traced here: 350 us
  waiting for transfers between devices  211 us (60%)
  Pallas kernels  81.6 us (23%)
  starting transfers between devices  47 us (13%)
  local copies, waits for them, and re-layouts  5.46 us (2%)
  other arithmetic  4.47 us (1%)
    all_to_all x1, waiting for transfers between devices, per_device(): lax.all_to_all(dx.reshape(2 * RING, 2 * most, width + SCORE), 'expert', 0...  84.1 us
    ppermute x1, waiting for transfers between devices, per_device(): minus1 = lax.ppermute(own, 'expert', down_ring)  33.2 us
    pallas_call x4, Pallas kernels, chunk_grads(): pl.pallas_call(body, out_shape=[jax.ShapeDtypeStruct((total_rows, n), BF)...  30.2 us
    ppermute x1, waiting for transfers between devices, per_device(): minus2 = lax.ppermute(minus1, 'expert', down_ring)  30 us
    all_to_all x4, starting transfers between devices, exchange(): lax.all_to_all(block, 'expert', 0, 0, tiled=True, axis_index_groups=PLANE...  21 us
    ppermute x1, waiting for transfers between devices, per_device(): minus3 = lax.ppermute(onward_down, 'expert', down_ring)  15.5 us
    ppermute x1, waiting for transfers between devices, per_device(): away = lax.ppermute(leaving, 'expert', ACROSS)  14.5 us
    pallas_call x4, Pallas kernels, pick_call(): pl.pallas_call(inner, grid=(width // TILE,), out_shape=[jax.ShapeDtypeStr...  14.3 us
  transfers between devices with their start and end apart: 17, of which 13 were waited for; matrix products, arithmetic and copies ran while one was open for 1% of the time, Pallas kernels for 20%

profile of v4, /device:TPU:2, one launch (start us, length us, event | category | flops | bytes accessed | tf_op | source)
XLA Modules:
  0.0 350.0 jit_solution(16884414769532972277)
XLA Ops:
  5.4 5.9 %collective-permute-start.2 = (bf16[528,2048]{1,0:T(8,128)(2,1)}, bf16[528,2048]{1,0:T(8,128)(2,1)}, u32[]{:S(2)}, u32[]{:S(2)}) collective-permute-start(bf16[528,2048]{1,0:T(8,128)(2,1)} %shard_map.128.refs_0_.refs_1_), channel_id=1, source_target_pairs={{0,28},{1,29},{2,30},{3,31},{4,0},{5,1},{6,2},{7,3},{8,4},{9,5},{1... | collective-permute-start | bytes 6488072 | tf_op jit(solution)/shard_map/ppermute | solution.py:411
  12.1 4.4 %collective-permute-done.4.refs_2_.place_ref = s32[256,2]{1,0:T(8,128)S(1)} collective-permute-done((s32[256,2]{1,0:T(8,128)S(1)}, s32[256,2]{1,0:T(8,128)S(1)}, u32[]{:S(2)}, u32[]{:S(2)}) %collective-permute-start.4) | collective-permute-done | bytes 2080 | tf_op jit(solution)/shard_map/ppermute | solution.py:406
  19.9 4.8 %all-to-all-start = ((bf16[4,64,2048]{2,1,0:T(8,128)(2,1)}), bf16[4,64,2048]{2,1,0:T(8,128)(2,1)}, u32[]{:S(2)}, u32[]{:S(2)}) async-start(bf16[4,64,2048]{2,1,0:T(8,128)(2,1)} %bitcast.85), calls=%async_computation | async-start | bytes 2097152 | tf_op jit(solution)/shard_map/all_to_all | solution.py:416
  24.7 33.2 %collective-permute-done.2.refs_1_.refs_3_ = bf16[528,2048]{1,0:T(8,128)(2,1)} collective-permute-done((bf16[528,2048]{1,0:T(8,128)(2,1)}, bf16[528,2048]{1,0:T(8,128)(2,1)}, u32[]{:S(2)}, u32[]{:S(2)}) %collective-permute-start.2) | collective-permute-done | bytes 2162720 | tf_op jit(solution)/shard_map/ppermute | solution.py:411
  65.4 5.0 %all-to-all-start.1 = ((bf16[4,128,2048]{2,1,0:T(8,128)(2,1)}), bf16[4,128,2048]{2,1,0:T(8,128)(2,1)}, u32[]{:S(2)}, u32[]{:S(2)}) async-start(bf16[4,128,2048]{2,1,0:T(8,128)(2,1)} %bitcast.83), calls=%async_computation.1 | async-start | bytes 4194304 | tf_op jit(solution)/shard_map/all_to_all | solution.py:416
  71.0 6.4 %shard_map.131 = (bf16[1024,2048]{1,0:T(8,128)(2,1)}, bf16[1024,2048]{1,0:T(8,128)(2,1)}, bf16[1024,384]{1,0:T(8,128)(2,1)}, bf16[1024,768]{1,0:T(8,128)(2,1)}, bf16[1024,2176]{1,0:T(8,128)(2,1)}) custom-call(s32[4]{0:T(128)} %pad_add_fusion.1.refs_0_, bf16[256,2048]{1,0:T(8,128)(2,1)} %bitcast.27.refs_1_, bf16[2048,384]{1,0:T(8,128)(2,1)} %bitcast.71, ...), custom_call_target="tpu_custom_call" | custom-call | flops 1 | bytes 1 | tf_op jit(solution)/shard_map/pallas_call | solution.py:313
  77.3 30.0 %collective-permute-done.3.refs_1_.refs_3_ = bf16[528,2048]{1,0:T(8,128)(2,1)} collective-permute-done((bf16[528,2048]{1,0:T(8,128)(2,1)}, bf16[528,2048]{1,0:T(8,128)(2,1)}, u32[]{:S(2)}, u32[]{:S(2)}) %collective-permute-start.3) | collective-permute-done | bytes 2162720 | tf_op jit(solution)/shard_map/ppermute | solution.py:413
  110.7 4.3 %shard_map.132.refs_4_ = bf16[768,2048]{1,0:T(8,128)(2,1)} custom-call(bf16[528,2048]{1,0:T(8,128)(2,1)} %collective-permute-done.1.refs_0_.refs_2_, bf16[528,2048]{1,0:T(8,128)(2,1)} %collective-permute-done.3.refs_1_.refs_3_, bf16[528,2048]{1,0:T(8,128)(2,1)} %collective-permute-done.1.refs_0_.refs_2_, ...), custom_call_target="tpu_custom_call" | custom-call | flops 1 | bytes 1 | tf_op jit(solution)/shard_map/pallas_call | solution.py:108
  115.0 5.2 %all-to-all-start.3 = ((bf16[4,192,2048]{2,1,0:T(8,128)(2,1)}), bf16[4,192,2048]{2,1,0:T(8,128)(2,1)}, u32[]{:S(2)}, u32[]{:S(2)}) async-start(bf16[4,192,2048]{2,1,0:T(8,128)(2,1)} %bitcast.70), calls=%async_computation.3 | async-start | bytes 6291456 | tf_op jit(solution)/shard_map/all_to_all | solution.py:416
  126.4 7.4 %shard_map.134 = (bf16[1024,2048]{1,0:T(8,128)(2,1)}, bf16[1024,2048]{1,0:T(8,128)(2,1)}, bf16[1024,384]{1,0:T(8,128)(2,1)}, bf16[1024,768]{1,0:T(8,128)(2,1)}, bf16[1024,2176]{1,0:T(8,128)(2,1)}) custom-call(s32[8]{0:T(128)} %stack.159.refs_0_, ...), custom_call_target="tpu_custom_call", output_to_operand_aliasing={{0}: (6, {}), {1}: (7, {}), {2}: (8, {}), {3}: (9, {}), {4}... | custom-call | flops 1 | bytes 1 | tf_op jit(solution)/shard_map/pallas_call | solution.py:313
  133.8 15.5 %collective-permute-done.6.down_ref = bf16[256,2048]{1,0:T(8,128)(2,1)} collective-permute-done((bf16[256,2048]{1,0:T(8,128)(2,1)}, bf16[256,2048]{1,0:T(8,128)(2,1)}, u32[]{:S(2)}, u32[]{:S(2)}) %collective-permute-start.6) | collective-permute-done | bytes 1048608 | tf_op jit(solution)/shard_map/ppermute | solution.py:470
  155.5 6.1 %all-to-all-start.2 = ((bf16[4,128,2048]{2,1,0:T(8,128)(2,1)}), bf16[4,128,2048]{2,1,0:T(8,128)(2,1)}, u32[]{:S(2)}, u32[]{:S(2)}) async-start(bf16[4,128,2048]{2,1,0:T(8,128)(2,1)} %bitcast.84), calls=%async_computation.2 | async-start | bytes 4194304 | tf_op jit(solution)/shard_map/all_to_all | solution.py:416
  168.5 7.4 %shard_map.137 = (bf16[1024,2048]{1,0:T(8,128)(2,1)}, bf16[1024,2048]{1,0:T(8,128)(2,1)}, bf16[1024,384]{1,0:T(8,128)(2,1)}, bf16[1024,768]{1,0:T(8,128)(2,1)}, bf16[1024,2176]{1,0:T(8,128)(2,1)}) custom-call(s32[8]{0:T(128)} %stack.168.refs_0_, ...), custom_call_target="tpu_custom_call", output_to_operand_aliasing={{0}: (7, {}), {1}: (8, {}), {2}: (9, {}), {3}: (10, {}), {4... | custom-call | flops 1 | bytes 1 | tf_op jit(solution)/shard_map/pallas_call | solution.py:313
  175.9 9.8 %all-to-all-done.2 = bf16[4,128,2048]{2,1,0:T(8,128)(2,1)} async-done(((bf16[4,128,2048]{2,1,0:T(8,128)(2,1)}), bf16[4,128,2048]{2,1,0:T(8,128)(2,1)}, u32[]{:S(2)}, u32[]{:S(2)}) %all-to-all-start.2) | async-done | bytes 2097184 | tf_op jit(solution)/shard_map/all_to_all | solution.py:416
  190.7 9.1 %shard_map.138 = (bf16[1024,2048]{1,0:T(8,128)(2,1)}, bf16[1024,2048]{1,0:T(8,128)(2,1)}, bf16[1024,384]{1,0:T(8,128)(2,1)}, bf16[1024,768]{1,0:T(8,128)(2,1)}, bf16[1024,2176]{1,0:T(8,128)(2,1)}) custom-call(s32[12]{0:T(128)} %stack.145.refs_0_, ...), custom_call_target="tpu_custom_call", output_to_operand_aliasing={{0}: (7, {}), {1}: (8, {}), {2}: (9, {}), {3}: (10, {}), {4... | custom-call | flops 1 | bytes 1 | tf_op jit(solution)/shard_map/pallas_call | solution.py:313
  199.8 4.9 %all-to-all-start.4 = ((bf16[16,64,2176]{2,1,0:T(8,128)(2,1)}), bf16[16,64,2176]{2,1,0:T(8,128)(2,1)}, u32[]{:S(2)}, u32[]{:S(2)}) async-start(bf16[16,64,2176]{2,1,0:T(8,128)(2,1)} %bitcast.69), calls=%async_computation.4 | async-start | bytes 8912896 | tf_op jit(solution)/shard_map/all_to_all | solution.py:493
  204.7 9.5 %shard_map.141 = (bf16[384,2048]{1,0:T(8,128)(2,1)}, bf16[2048,768]{1,0:T(8,128)(2,1)}) custom-call(bf16[1024,2048]{1,0:T(8,128)(2,1)} %get-tuple-element.53.x_ref, bf16[1024,768]{1,0:T(8,128)(2,1)} %get-tuple-element.54.d_ref, bf16[1024,384]{1,0:T(8,128)(2,1)} %get-tuple-element.55.hidden_ref, bf16[1024,2048]{1,0:T(8,128)(2,1)} %get-tuple-element.56.g_ref), custom_call_target="tpu_custom_call" | custom-call | flops 1 | bytes 1 | tf_op jit(solution)/shard_map/pallas_call | solution.py:350
  214.2 4.9 %collective-permute-start.10 = (bf16[2048,768]{1,0:T(8,128)(2,1)}, bf16[2048,768]{1,0:T(8,128)(2,1)}, u32[]{:S(2)}, u32[]{:S(2)}) collective-permute-start(bf16[2048,768]{1,0:T(8,128)(2,1)} %get-tuple-element.57.a_ref), channel_id=1, source_target_pairs={{0,224},{32,192},{64,160},{96,128},{128,96},{160,64},{192,32},{224... | collective-permute-start | bytes 9437192 | tf_op jit(solution)/shard_map/ppermute | solution.py:491
  220.4 84.1 %all-to-all-done.4 = bf16[16,64,2176]{2,1,0:T(8,128)(2,1)} async-done(((bf16[16,64,2176]{2,1,0:T(8,128)(2,1)}), bf16[16,64,2176]{2,1,0:T(8,128)(2,1)}, u32[]{:S(2)}, u32[]{:S(2)}) %all-to-all-start.4) | async-done | bytes 4456480 | tf_op jit(solution)/shard_map/all_to_all | solution.py:493
  304.6 4.9 %shard_map.140.refs_0_ = bf16[256,2176]{1,0:T(8,128)(2,1)} custom-call(s32[2]{0:T(128)} %pad_add_fusion.2.info_ref, s32[256,2]{1,0:T(8,128)} %copy-done.1, bf16[1024,2176]{1,0:T(8,128)(2,1)} %bitcast.54.back_ref), custom_call_target="tpu_custom_call" | custom-call | flops 1 | bytes 1 | tf_op jit(solution)/shard_map/pallas_call | solution.py:231
  310.5 5.0 %shard_map.139 = bf16[256,2176]{1,0:T(8,128)(2,1)} custom-call(s32[2]{0:T(128)} %pad_add_fusion.info_ref, s32[256,2]{1,0:T(8,128)} %copy-done.2, bf16[1024,2176]{1,0:T(8,128)(2,1)} %bitcast.54.back_ref), custom_call_target="tpu_custom_call" | custom-call | flops 1 | bytes 1 | tf_op jit(solution)/shard_map/pallas_call | solution.py:231
  315.4 7.3 %collective-permute-done.11.b_ref = bf16[384,2048]{1,0:T(8,128)(2,1)} collective-permute-done((bf16[384,2048]{1,0:T(8,128)(2,1)}, bf16[384,2048]{1,0:T(8,128)(2,1)}, u32[]{:S(2)}, u32[]{:S(2)}) %collective-permute-start.11) | collective-permute-done | bytes 1572896 | tf_op jit(solution)/shard_map/ppermute | solution.py:490
  326.7 5.0 %shard_map.143 = (bf16[2048,384]{1,0:T(8,128)(2,1)}, bf16[2048,384]{1,0:T(8,128)(2,1)}) custom-call(bf16[2048,768]{1,0:T(8,128)(2,1)} %get-tuple-element.57.a_ref, bf16[2048,768]{1,0:T(8,128)(2,1)} %collective-permute-done.10.b_ref, bf16[384,2048]{1,0:T(8,128)(2,1)} %shard_map.142.refs_0_), custom_call_target="tpu_custom_call" | custom-call | flops 1 | bytes 1 | tf_op jit(solution)/shard_map/pallas_call | solution.py:379
  331.7 14.5 %collective-permute-done.9 = bf16[256,2176]{1,0:T(8,128)(2,1)} collective-permute-done((bf16[256,2176]{1,0:T(8,128)(2,1)}, bf16[256,2176]{1,0:T(8,128)(2,1)}, u32[]{:S(2)}, u32[]{:S(2)}) %collective-permute-start.9) | collective-permute-done | bytes 1114144 | tf_op jit(solution)/shard_map/ppermute | solution.py:502
  (50 shorter events, 54.9 us)
Async XLA Ops:
  2.1 9.2 %copy-start.4 = (s32[1,256,2]{1,2,0:T(2,128)S(1)}, s32[1,256,2]{1,2,0:T(2,128)}, u32[]{:S(2)}) copy-start(s32[1,256,2]{1,2,0:T(2,128)} %param.12) | copy-start | bytes 6148
  5.4 52.5 %collective-permute-start.2 = (bf16[528,2048]{1,0:T(8,128)(2,1)}, bf16[528,2048]{1,0:T(8,128)(2,1)}, u32[]{:S(2)}, u32[]{:S(2)}) collective-permute-start(bf16[528,2048]{1,0:T(8,128)(2,1)} %shard_map.128.refs_0_.refs_1_), channel_id=1, source_target_pairs={{0,28},{1,29},{2,30},{3,31},{4,0},{5,1},{6,2},{7,3},{8,4},{9,5},{1... | collective-permute-start | bytes 6488072 | tf_op jit(solution)/shard_map/ppermute | solution.py:411
  11.3 50.3 %collective-permute-start = (bf16[528,2048]{1,0:T(8,128)(2,1)}, bf16[528,2048]{1,0:T(8,128)(2,1)}, u32[]{:S(2)}, u32[]{:S(2)}) collective-permute-start(bf16[528,2048]{1,0:T(8,128)(2,1)} %shard_map.128.refs_0_.refs_1_), channel_id=1, source_target_pairs={{0,4},{1,5},{2,6},{3,7},{4,8},{5,9},{6,10},{7,11},{8,12},{9,13},{1... | collective-permute-start | bytes 6488072 | tf_op jit(solution)/shard_map/ppermute | solution.py:410
  11.4 53.9 %copy-start.2 = (s32[256,2]{1,0:T(8,128)}, s32[256,2]{1,0:T(8,128)S(1)}, u32[]{:S(2)}) copy-start(s32[256,2]{1,0:T(8,128)S(1)} %bitcast_add_fusion.place_ref) | copy-start | bytes 6148
  11.5 5.1 %collective-permute-start.4 = (s32[256,2]{1,0:T(8,128)S(1)}, s32[256,2]{1,0:T(8,128)S(1)}, u32[]{:S(2)}, u32[]{:S(2)}) collective-permute-start(s32[256,2]{1,0:T(8,128)S(1)} %bitcast_add_fusion.place_ref), channel_id=1, source_target_pairs={{0,2},{1,3},{2,0},{3,1},{4,6},{5,7},{6,4},{7,5},{8,10},{9,11},{10,... | collective-permute-start | bytes 6152 | tf_op jit(solution)/shard_map/ppermute | solution.py:406
  16.5 0.7 copy-start.1
  19.9 45.4 %all-to-all-start = ((bf16[4,64,2048]{2,1,0:T(8,128)(2,1)}), bf16[4,64,2048]{2,1,0:T(8,128)(2,1)}, u32[]{:S(2)}, u32[]{:S(2)}) async-start(bf16[4,64,2048]{2,1,0:T(8,128)(2,1)} %bitcast.85), calls=%async_computation | async-start | bytes 2097152 | tf_op jit(solution)/shard_map/all_to_all | solution.py:416
  57.9 49.4 %collective-permute-start.3 = (bf16[528,2048]{1,0:T(8,128)(2,1)}, bf16[528,2048]{1,0:T(8,128)(2,1)}, u32[]{:S(2)}, u32[]{:S(2)}) collective-permute-start(bf16[528,2048]{1,0:T(8,128)(2,1)} %collective-permute-done.2.refs_1_.refs_3_), channel_id=1, source_target_pairs={{0,28},{1,29},{2,30},{3,31},{4,0},{5,1},{6,2},{7,3},{8,4},{9,5},{1... | collective-permute-start | bytes 6488072 | tf_op jit(solution)/shard_map/ppermute | solution.py:413
  61.6 49.1 %collective-permute-start.1 = (bf16[528,2048]{1,0:T(8,128)(2,1)}, bf16[528,2048]{1,0:T(8,128)(2,1)}, u32[]{:S(2)}, u32[]{:S(2)}) collective-permute-start(bf16[528,2048]{1,0:T(8,128)(2,1)} %collective-permute-done.refs_0_.refs_2_), channel_id=1, source_target_pairs={{0,4},{1,5},{2,6},{3,7},{4,8},{5,9},{6,10},{7,11},{8,12},{9,13},{1... | collective-permute-start | bytes 6488072 | tf_op jit(solution)/shard_map/ppermute | solution.py:412
  65.4 49.6 %all-to-all-start.1 = ((bf16[4,128,2048]{2,1,0:T(8,128)(2,1)}), bf16[4,128,2048]{2,1,0:T(8,128)(2,1)}, u32[]{:S(2)}, u32[]{:S(2)}) async-start(bf16[4,128,2048]{2,1,0:T(8,128)(2,1)} %bitcast.83), calls=%async_computation.1 | async-start | bytes 4194304 | tf_op jit(solution)/shard_map/all_to_all | solution.py:416
  115.0 40.5 %all-to-all-start.3 = ((bf16[4,192,2048]{2,1,0:T(8,128)(2,1)}), bf16[4,192,2048]{2,1,0:T(8,128)(2,1)}, u32[]{:S(2)}, u32[]{:S(2)}) async-start(bf16[4,192,2048]{2,1,0:T(8,128)(2,1)} %bitcast.70), calls=%async_computation.3 | async-start | bytes 6291456 | tf_op jit(solution)/shard_map/all_to_all | solution.py:416
  123.7 25.5 %collective-permute-start.6 = (bf16[256,2048]{1,0:T(8,128)(2,1)}, bf16[256,2048]{1,0:T(8,128)(2,1)}, u32[]{:S(2)}, u32[]{:S(2)}) collective-permute-start(bf16[256,2048]{1,0:T(8,128)(2,1)} %get-tuple-element.35), channel_id=1, source_target_pairs={{0,28},{1,29},{2,30},{3,31},{4,0},{5,1},{6,2},{7,3},{8,4},{9,5},{1... | collective-permute-start | bytes 3145736 | tf_op jit(solution)/shard_map/ppermute | solution.py:470
  124.0 26.7 %collective-permute-start.5 = (bf16[256,2048]{1,0:T(8,128)(2,1)}, bf16[256,2048]{1,0:T(8,128)(2,1)}, u32[]{:S(2)}, u32[]{:S(2)}) collective-permute-start(bf16[256,2048]{1,0:T(8,128)(2,1)} %get-tuple-element.34.refs_5_), channel_id=1, source_target_pairs={{0,4},{1,5},{2,6},{3,7},{4,8},{5,9},{6,10},{7,11},{8,12},{9,13},{1... | collective-permute-start | bytes 3145736 | tf_op jit(solution)/shard_map/ppermute | solution.py:469
  155.5 30.2 %all-to-all-start.2 = ((bf16[4,128,2048]{2,1,0:T(8,128)(2,1)}), bf16[4,128,2048]{2,1,0:T(8,128)(2,1)}, u32[]{:S(2)}, u32[]{:S(2)}) async-start(bf16[4,128,2048]{2,1,0:T(8,128)(2,1)} %bitcast.84), calls=%async_computation.2 | async-start | bytes 4194304 | tf_op jit(solution)/shard_map/all_to_all | solution.py:416
  164.3 25.6 %collective-permute-start.8 = (bf16[128,2048]{1,0:T(8,128)(2,1)}, bf16[128,2048]{1,0:T(8,128)(2,1)S(1)}, u32[]{:S(2)}, u32[]{:S(2)}) collective-permute-start(bf16[128,2048]{1,0:T(8,128)(2,1)} %get-tuple-element.42), channel_id=1, source_target_pairs={{0,24},{1,25},{2,26},{3,27},{4,28},{5,29},{6,30},{7,31},{8,0},{9,1... | collective-permute-start | bytes 1572872 | tf_op jit(solution)/shard_map/ppermute | solution.py:475
  164.3 26.3 %collective-permute-start.7 = (bf16[128,2048]{1,0:T(8,128)(2,1)}, bf16[128,2048]{1,0:T(8,128)(2,1)}, u32[]{:S(2)}, u32[]{:S(2)}) collective-permute-start(bf16[128,2048]{1,0:T(8,128)(2,1)} %get-tuple-element.41.refs_6_), channel_id=1, source_target_pairs={{0,8},{1,9},{2,10},{3,11},{4,12},{5,13},{6,14},{7,15},{8,16},{9,17... | collective-permute-start | bytes 1572872 | tf_op jit(solution)/shard_map/ppermute | solution.py:474
  189.9 0.8 copy-start
  199.8 104.7 %all-to-all-start.4 = ((bf16[16,64,2176]{2,1,0:T(8,128)(2,1)}), bf16[16,64,2176]{2,1,0:T(8,128)(2,1)}, u32[]{:S(2)}, u32[]{:S(2)}) async-start(bf16[16,64,2176]{2,1,0:T(8,128)(2,1)} %bitcast.69), calls=%async_computation.4 | async-start | bytes 8912896 | tf_op jit(solution)/shard_map/all_to_all | solution.py:493
  214.2 112.5 %collective-permute-start.10 = (bf16[2048,768]{1,0:T(8,128)(2,1)}, bf16[2048,768]{1,0:T(8,128)(2,1)}, u32[]{:S(2)}, u32[]{:S(2)}) collective-permute-start(bf16[2048,768]{1,0:T(8,128)(2,1)} %get-tuple-element.57.a_ref), channel_id=1, source_target_pairs={{0,224},{32,192},{64,160},{96,128},{128,96},{160,64},{192,32},{224... | collective-permute-start | bytes 9437192 | tf_op jit(solution)/shard_map/ppermute | solution.py:491
  219.1 103.7 %collective-permute-start.11 = (bf16[384,2048]{1,0:T(8,128)(2,1)}, bf16[384,2048]{1,0:T(8,128)(2,1)}, u32[]{:S(2)}, u32[]{:S(2)}) collective-permute-start(bf16[384,2048]{1,0:T(8,128)(2,1)} %get-tuple-element.58.a_ref), channel_id=1, source_target_pairs={{0,224},{32,192},{64,160},{96,128},{128,96},{160,64},{192,32},{224... | collective-permute-start | bytes 4718600 | tf_op jit(solution)/shard_map/ppermute | solution.py:490
  309.5 36.7 %collective-permute-start.9 = (bf16[256,2176]{1,0:T(8,128)(2,1)}, bf16[256,2176]{1,0:T(8,128)(2,1)}, u32[]{:S(2)}, u32[]{:S(2)}) collective-permute-start(bf16[256,2176]{1,0:T(8,128)(2,1)} %shard_map.140.refs_0_), channel_id=1, source_target_pairs={{0,2},{1,3},{2,0},{3,1},{4,6},{5,7},{6,4},{7,5},{8,10},{9,11},{10,... | collective-permute-start | bytes 3342344 | tf_op jit(solution)/shard_map/ppermute | solution.py:502
  348.0 1.4 copy-start.3
